TPU v7x, 32 devices: a whole 2x2x4 slice. The times are simulated.
32 devices in a mesh: groups: 2 (over y), visit: 4 (over z), strip: 2 (over x), band: 2 (over core).
Axes of the slice: x: 2, y: 2, z: 4, core: 2. Of those that a mesh axis runs over, the one named last changes fastest.
Arguments:
- images: bfloat16 [2, 128, 128, 256], P('band', ('groups', 'visit'), 'strip'), parts along dimension 1, may hold values from -8 to 8
- mask_bits: int32 [2, 128, 128, 256], P('band', ('groups', 'visit'), 'strip'), parts along dimension 1, may hold values from 0 to 15
- visit_weight: bfloat16 [2, 128], P('band', ('groups', 'visit')), parts along dimension 1, may hold values from 1 to 4
- intersection: int32 [128, 1], P(('groups', 'visit')), parts along dimension 0, may hold values from 0 to 3, as said below
- patch_owner: int32 [8], P('groups'), parts along dimension 0, may hold values from 0 to 3, each once
Outputs:
- coadd_image: bfloat16 [2, 8, 128, 256], P('band', ('groups', 'visit'), 'strip'), parts along dimension 1
- difference: bfloat16 [2, 128, 128, 256], P('band', ('groups', 'visit'), 'strip'), parts along dimension 1
There are 2 independent parts, one for each index of `groups`. A program takes and returns all parts, laid end to end along the dimension named above; each array names one. Nothing has to cross between parts.
Inputs may be any that keep to these rules, and one draw needn't show every extreme that they name: `intersection`: row j names the patch that piece j intersections. The 16 pieces of one visit index intersect 16 // 8 distinct patches, exactly 8 pieces each; one patch is intersected by 8 pieces of every visit index, and every patch is intersected by some piece. `patch_owner`: A permutation of the patches.
All inputs are finite; a program needn't handle non-finite values.
Results may differ from a plain program's by a relative error of at most 0.0071.
Values may be sent and summed in bfloat16 or wider, within the bound.
No kernel may reach another device: no remote copies, remote signals or barrier semaphores. Data moves between devices by JAX's collectives and lax.ppermute only.
A program may use at most 64 MiB of HBM per device.

v0:
```python
import functools

import jax
import jax.numpy as jnp
import ml_dtypes
import numpy as np
from jax import lax
from jax.experimental import pallas as pl
from jax.experimental.pallas import tpu as pltpu
from jax.sharding import PartitionSpec as P

BASES = 6
HALF = 9
TILE = 16
basis_rows = (0, 0, 1, 0, 2, 1)
basis_cols = (0, 1, 0, 2, 0, 1)
VMEM_LIMIT = 48 * 1024 * 1024

VMEM = pl.BlockSpec(memory_space=pltpu.VMEM)
SMEM = pl.BlockSpec(memory_space=pltpu.SMEM)


def tap_rows():
    offsets = np.arange(2 * HALF + 1).astype(np.float64) - HALF
    gaussian = np.exp(-offsets * offsets / 18.0)
    squared = gaussian * gaussian
    centre = np.sum(offsets * offsets * squared) / np.sum(squared)
    table = np.stack([gaussian, offsets * gaussian, (offsets * offsets - centre) * gaussian])
    table = table / np.sqrt(np.sum(table * table, axis=1, keepdims=True))
    return table.astype(ml_dtypes.bfloat16)


def across_matrices(cols):
    taps = tap_rows()
    distance = np.arange(cols)[:, None] - np.arange(cols)[None, :] + HALF
    inside = (distance >= 0) & (distance <= 2 * HALF)
    return np.where(inside[None], taps[:, np.clip(distance, 0, 2 * HALF)], 0).astype(ml_dtypes.bfloat16)


def vertical_matrix(rows, sources):
    taps = tap_rows()
    distance = np.asarray(sources)[None, :] - np.arange(rows)[:, None] + HALF
    inside = (distance >= 0) & (distance <= 2 * HALF)
    table = np.where(inside[None], taps[:, np.clip(distance, 0, 2 * HALF)], 0)
    return table.reshape(3 * rows, len(sources)).astype(ml_dtypes.bfloat16)


def unusable(mask):
    return jnp.bitwise_and(mask, 3) == 3


def partial_kernel(slots, cap, ids_ref, weight_ref, image_ref, mask_ref, message_ref, order_ref):
    pieces, rows, cols = image_ref.shape
    ids = [ids_ref[j] for j in range(pieces)]
    for j in range(pieces):
        place = jnp.int32(0)
        for i in range(pieces):
            if i < j:
                place = place + (ids[i] <= ids[j]).astype(jnp.int32)
            elif i > j:
                place = place + (ids[i] < ids[j]).astype(jnp.int32)
        order_ref[place] = j
    for slot in range(slots):
        for first in range(0, rows, TILE):
            numerator = jnp.zeros((TILE, cols), jnp.float32)
            denominator = jnp.zeros((TILE, cols), jnp.float32)
            for k in range(cap):
                j = order_ref[slot * cap + k]
                bad = unusable(mask_ref[j, first : first + TILE, :])
                weight = jnp.where(bad, 0.0, weight_ref[j])
                denominator = denominator + weight
                numerator = numerator + weight * image_ref[j, first : first + TILE, :].astype(jnp.float32)
            at = slot * 2 * rows + first
            message_ref[at : at + TILE, :] = numerator.astype(jnp.bfloat16)
            message_ref[at + rows : at + rows + TILE, :] = denominator.astype(jnp.bfloat16)
    line = lax.broadcasted_iota(jnp.int32, (TILE, cols), 0)
    labels = jnp.zeros((TILE, cols), jnp.float32)
    for slot in range(slots):
        labels = jnp.where(line == slot, ids_ref[order_ref[slot * cap]].astype(jnp.float32), labels)
    message_ref[slots * 2 * rows :, :] = labels.astype(jnp.bfloat16)


def sort_kernel(slots, cap, order_ref, image_ref, mask_ref, usable_ref, masked_ref):
    rows, cols = image_ref.shape[1:]
    for slot in range(slots):
        for k in range(cap):
            j = order_ref[slot * cap + k]
            for g in range(rows // TILE):
                lines = slice(g * TILE, (g + 1) * TILE)
                usable = jnp.where(unusable(mask_ref[j, lines, :]), 0.0, 1.0).astype(jnp.bfloat16)
                at = (slot, slice(k * TILE, (k + 1) * TILE), slice(g * cols, (g + 1) * cols))
                usable_ref[at] = usable
                masked_ref[at] = usable * image_ref[j, lines, :]


def combine_kernel(slots, count, info_ref, owner_ref, *refs):
    own_ref = refs[0]
    sources, (template_ref, edge_ref, coadd_ref), total_ref = refs[1:-4], refs[-4:-1], refs[-1]
    rows, cols = coadd_ref.shape
    base = slots * 2 * rows
    mine = jnp.int32(0)
    for p in range(owner_ref.shape[0]):
        mine = jnp.where(owner_ref[p] == info_ref[0], p, mine)
    mine = mine.astype(jnp.float32)
    own_labels = own_ref[base:, :].astype(jnp.float32)

    def picks(labels, slot):
        label = labels[slot : slot + 1, :]
        hits = [label == own_labels[t : t + 1, :] for t in range(slots)] + [label == mine]
        return [hit.astype(jnp.float32) for hit in hits]

    def finish(target, numerator, denominator, first):
        coadd = (numerator / jnp.maximum(denominator, 1.0)).astype(jnp.bfloat16)
        if target < slots:
            template_ref[target, first : first + TILE, :] = coadd
        else:
            coadd_ref[first : first + TILE, :] = coadd

    if len(sources) == count:
        hits = [
            [picks(ref[base:, :].astype(jnp.float32), slot) for slot in range(slots)]
            for ref in (own_ref,) + tuple(sources[1:])
        ]
        refs_all = (own_ref,) + tuple(sources[1:])
        for first in range(0, rows, TILE):
            sums = [[jnp.zeros((TILE, cols), jnp.float32) for _ in range(2)] for _ in range(slots + 1)]
            for d, ref in enumerate(refs_all):
                for slot in range(slots):
                    for kind in range(2):
                        at = (slot * 2 + kind) * rows + first
                        value = ref[at : at + TILE, :].astype(jnp.float32)
                        for t in range(slots + 1):
                            if d == 0 and t < slots:
                                if t == slot:
                                    sums[t][kind] = sums[t][kind] + value
                            else:
                                sums[t][kind] = sums[t][kind] + hits[d][slot][t] * value
            for t in range(slots + 1):
                finish(t, sums[t][0], sums[t][1], first)
    else:
        stacked = sources[0]
        total_ref[...] = jnp.zeros_like(total_ref)

        def add_source(d, carry):
            labels = stacked[d, base:, :].astype(jnp.float32)
            for slot in range(slots):
                pick = picks(labels, slot)
                for kind in range(2):
                    at = (slot * 2 + kind) * rows
                    value = stacked[d, at : at + rows, :].astype(jnp.float32)
                    for t in range(slots + 1):
                        total_ref[t, kind] += pick[t] * value
            return carry

        lax.fori_loop(0, count, add_source, 0)
        for t in range(slots + 1):
            for first in range(0, rows, TILE):
                finish(t, total_ref[t, 0, first : first + TILE, :], total_ref[t, 1, first : first + TILE, :], first)
    edges = edge_ref.shape[1] // TILE
    if edges == 1:
        first = pl.multiple_of(jnp.where(info_ref[1] == 0, rows - TILE, 0), TILE)
        edge_ref[...] = template_ref[:, pl.ds(first, TILE), :]
    else:
        edge_ref[:, :TILE, :] = template_ref[:, :TILE, :]
        edge_ref[:, TILE:, :] = template_ref[:, rows - TILE :, :]


def normal_kernel(slots, cap, info_ref, template_ref, *refs):
    halo_refs, (vertical_ref, across_ref, usable_ref, masked_ref) = refs[:-8], refs[-8:-4]
    basis_ref, sums_ref, smooth_ref, left_ref = refs[-4:]
    rows, cols = template_ref.shape[1:]
    tiles = rows // TILE
    which = info_ref[1] if vertical_ref.shape[0] > 1 else 0
    vertical = vertical_ref[which]
    for slot in range(slots):
        extended = jnp.concatenate([template_ref[slot]] + [ref[slot] for ref in halo_refs], axis=0)
        smooth = jnp.dot(vertical, extended, preferred_element_type=jnp.float32)
        for k in range(3):
            smooth_ref[k, slot] = smooth[k * rows : (k + 1) * rows].astype(jnp.bfloat16)
    for c in range(3):
        users = [a for a in range(BASES) if basis_cols[a] == c]
        for slot in range(slots):
            stacked = jnp.concatenate([smooth_ref[basis_rows[a], slot] for a in users], axis=0)
            planes = jnp.dot(stacked, across_ref[c], preferred_element_type=jnp.float32).astype(jnp.bfloat16)
            for n, a in enumerate(users):
                for g in range(tiles):
                    at = n * rows + g * TILE
                    basis_ref[slot, a * TILE : (a + 1) * TILE, g * cols : (g + 1) * cols] = planes[at : at + TILE]
    group = cap * TILE
    height = BASES * group + group
    for slot in range(slots):
        for a in range(BASES):
            plane = basis_ref[slot, a * TILE : (a + 1) * TILE, :]
            for k in range(cap):
                at = a * group + k * TILE
                left_ref[at : at + TILE, :] = plane * usable_ref[slot, k * TILE : (k + 1) * TILE, :]
        left_ref[BASES * group :, :] = masked_ref[slot]
        product = lax.dot_general(
            left_ref[...], basis_ref[slot], (((1,), (1,)), ((), ())), preferred_element_type=jnp.float32
        )
        width = product.shape[1]
        line = lax.broadcasted_iota(jnp.int32, (TILE, width), 0)
        lane = lax.broadcasted_iota(jnp.int32, (TILE, width), 1)
        same = line == lane % TILE
        product = jnp.where(same[None], product.reshape(height // TILE, TILE, width), 0.0)
        product = jnp.sum(product, axis=1)
        product = jnp.concatenate([product, jnp.zeros((height // TILE, 128 - width), jnp.float32)], axis=1)
        for step in (1, 2, 4, 8):
            product = product + pltpu.roll(product, 128 - step, 1)
        lanes = lax.broadcasted_iota(jnp.int32, product.shape, 1)
        product = jnp.where(lanes % TILE == 0, product, 0.0)
        packed = product[:cap]
        for a in range(1, BASES + 1):
            packed = packed + pltpu.roll(product[a * cap : (a + 1) * cap], a, 1)
        sums_ref[slot * cap : (slot + 1) * cap, :] = packed


def fit_kernel(slots, cap, order_ref, *refs):
    sums_refs, (basis_ref, image_ref, difference_ref) = refs[:-3], refs[-3:]
    rows, cols = image_ref.shape[1:]
    tiles = rows // TILE
    total = sums_refs[0][...]
    for ref in sums_refs[1:]:
        total = total + ref[...]
    pieces = total.shape[0]
    lanes = lax.broadcasted_iota(jnp.int32, (pieces, 128), 1)
    starts = lanes % TILE == 0
    table = []
    for c in range(BASES + 1):
        line = total if c == 0 else pltpu.roll(total, 128 - c, 1)
        line = jnp.where(starts, line, 0.0)
        if c < BASES:
            line = line + jnp.where(lanes == c * TILE, 1.0, 0.0)
        table.append(line)
    for k in range(BASES):
        at = k * TILE
        pivot = table[k]
        inverse = 1.0 / pivot[:, at : at + 1]
        for c in range(k + 1, BASES + 1):
            ratio = table[c][:, at : at + 1] * inverse
            table[c] = jnp.where(lanes == at, ratio, table[c] - pivot * ratio)
    spread = table[BASES]
    for step in (1, 2, 4, 8):
        spread = spread + pltpu.roll(spread, step, 1)
    line = lax.broadcasted_iota(jnp.int32, (TILE, 128), 0)
    lane = lax.broadcasted_iota(jnp.int32, (TILE, 128), 1)
    same = (line == lane % TILE) & (lane < BASES * TILE)
    for slot in range(slots):
        blocks = [
            jnp.where(same, spread[slot * cap + k : slot * cap + k + 1, :], 0.0) for k in range(cap)
        ]
        exact = jnp.concatenate(blocks, axis=0)[:, : BASES * TILE]
        high = exact.astype(jnp.bfloat16)
        low = (exact - high.astype(jnp.float32)).astype(jnp.bfloat16)
        basis = basis_ref[slot]
        fitted = jnp.dot(high, basis, preferred_element_type=jnp.float32) + jnp.dot(
            low, basis, preferred_element_type=jnp.float32
        )
        for k in range(cap):
            j = order_ref[slot * cap + k]
            for g in range(tiles):
                part = fitted[k * TILE : (k + 1) * TILE, g * cols : (g + 1) * cols]
                image = image_ref[j, g * TILE : (g + 1) * TILE, :].astype(jnp.float32)
                difference_ref[j, g * TILE : (g + 1) * TILE, :] = (image - part).astype(jnp.bfloat16)


def call(kernel, name, outs, in_specs, out_specs, args, scratch=(), flops=0, size=0):
    return pl.pallas_call(
        kernel,
        out_shape=outs,
        in_specs=in_specs,
        out_specs=out_specs,
        scratch_shapes=list(scratch),
        name=name,
        compiler_params=pltpu.CompilerParams(vmem_limit_bytes=VMEM_LIMIT),
        cost_estimate=pl.CostEstimate(flops=flops, bytes_accessed=size, transcendentals=0),
    )(*args)


def body(images, mask_bits, visit_weight, intersection, patch_owner):
    visits = lax.axis_size("visit")
    strips = lax.axis_size("strip")
    _, pieces, rows, cols = images.shape
    slots = visits // 2
    cap = pieces // slots
    tiles = rows // TILE
    shape = jax.ShapeDtypeStruct
    bf16, f32 = jnp.bfloat16, jnp.float32
    image = images[0]
    mask = mask_bits[0]
    ids = intersection[:, 0]
    info = jnp.stack([lax.axis_index("visit"), lax.axis_index("strip")]).astype(jnp.int32)
    label_rows = -(-slots // TILE) * TILE
    message_rows = slots * 2 * rows + label_rows

    message, order = call(
        functools.partial(partial_kernel, slots, cap),
        "partial_sums",
        (shape((message_rows, cols), bf16), shape((pieces,), jnp.int32)),
        [SMEM, SMEM, VMEM, VMEM],
        (VMEM, SMEM),
        (ids, visit_weight[0].astype(f32), image, mask),
        size=2 << 20,
    )
    if visits <= 4:
        received = [
            lax.ppermute(message, "visit", [(i, (i + shift) % visits) for i in range(visits)])
            for shift in range(1, visits)
        ]
        sources = [message] + received
    else:
        sources = [lax.all_gather(message, "visit")]
    usable, masked = call(
        functools.partial(sort_kernel, slots, cap),
        "sorted_usable",
        (shape((slots, cap * TILE, tiles * cols), bf16),) * 2,
        [SMEM, VMEM, VMEM],
        (VMEM, VMEM),
        (order, image, mask),
        size=3 << 20,
    )
    edges = 1 if strips == 2 else 2
    stacked = len(sources) == 1
    template, edge, coadd = call(
        functools.partial(combine_kernel, slots, visits),
        "combine",
        (shape((slots, rows, cols), bf16), shape((slots, edges * TILE, cols), bf16), shape((rows, cols), bf16)),
        [SMEM, SMEM] + [VMEM] * (len(sources) + 1),
        (VMEM,) * 3,
        (info, patch_owner, message, *sources),
        scratch=[pltpu.VMEM((slots + 1, 2, rows, cols) if stacked else (1, 2, TILE, cols), f32)],
        size=1 << 20,
    )
    if strips == 2:
        halos = [lax.ppermute(edge, "strip", [(0, 1), (1, 0)])]
        inside = list(range(rows))
        below = inside + list(range(rows, rows + TILE))
        above = inside + list(range(-TILE, 0))
        vertical = np.stack([vertical_matrix(rows, below), vertical_matrix(rows, above)])
    else:
        halos = [
            lax.ppermute(edge[:, TILE:], "strip", [(i, i + 1) for i in range(strips - 1)]),
            lax.ppermute(edge[:, :TILE], "strip", [(i + 1, i) for i in range(strips - 1)]),
        ]
        around = list(range(rows)) + list(range(-TILE, 0)) + list(range(rows, rows + TILE))
        vertical = vertical_matrix(rows, around)[None]
    basis, sums = call(
        functools.partial(normal_kernel, slots, cap),
        "normal_equations",
        (shape((slots, BASES * TILE, tiles * cols), bf16), shape((pieces, 128), f32)),
        [SMEM] + [VMEM] * (len(halos) + 5),
        (VMEM, VMEM),
        (info, template, *halos, jnp.asarray(vertical), jnp.asarray(across_matrices(cols)), usable, masked),
        scratch=[
            pltpu.VMEM((3, slots, rows, cols), bf16),
            pltpu.VMEM(((BASES + 1) * cap * TILE, tiles * cols), bf16),
        ],
        size=2 << 20,
    )
    if strips == 2:
        totals = [sums, lax.ppermute(sums, "strip", [(0, 1), (1, 0)])]
    else:
        totals = [lax.psum(sums, "strip")]
    difference = call(
        functools.partial(fit_kernel, slots, cap),
        "fit",
        shape((pieces, rows, cols), bf16),
        [SMEM] + [VMEM] * (len(totals) + 2),
        VMEM,
        (order, *totals, basis, image),
        size=2 << 20,
    )
    return (coadd[None, None], difference[None])


def solution(mesh):
    in_specs = (
        P("band", ("groups", "visit"), "strip", None),
        P("band", ("groups", "visit"), "strip", None),
        P("band", ("groups", "visit")),
        P(("groups", "visit"), None),
        P("groups"),
    )
    out_specs = (
        P("band", ("groups", "visit"), "strip", None),
        P("band", ("groups", "visit"), "strip", None),
    )
    return jax.shard_map(body, mesh=mesh, in_specs=in_specs, out_specs=out_specs, check_vma=False)
```

profile of v0, /device:TPU:0, one launch (start us, length us, event | category | flops | bytes accessed | tf_op | source)
XLA Modules:
  0.0 36.6 jit_solution(11473936296419287308)
XLA Ops:
  0.6 0.7 %bitcast_convert_fusion.weight_ref = f32[16]{0:T(128)S(1)} fusion(bf16[1,16]{1,0:T(2,128)(2,1)} %param.9), kind=kLoop, calls=%fused_computation.1 | loop fusion | flops 16 | bytes 96 | tf_op jit(solution)/shard_map/convert_element_type | solution.py:302
  1.3 0.7 %copy-done.6 = s32[16,1]{0,1:T(1,128)S(1)} copy-done((s32[16,1]{0,1:T(1,128)S(1)}, s32[16,1]{0,1:T(1,128)}, u32[]{:S(2)}) %copy-start.6) | copy-done | bytes 88
  1.9 1.0 %copy-done = bf16[1,16,64,256]{3,2,1,0:T(8,128)(2,1)S(1)} copy-done((bf16[1,16,64,256]{3,2,1,0:T(8,128)(2,1)S(1)}, bf16[1,16,64,256]{3,2,1,0:T(8,128)(2,1)}, u32[]{:S(2)}) %copy-start) | copy-done | bytes 524312
  3.0 1.2 %copy-done.2 = s32[1,16,64,256]{3,2,1,0:T(8,128)S(1)} copy-done((s32[1,16,64,256]{3,2,1,0:T(8,128)S(1)}, s32[1,16,64,256]{3,2,1,0:T(8,128)}, u32[]{:S(2)}) %copy-start.2) | copy-done | bytes 1048600
  4.2 1.6 %partial_sums.1 = (bf16[272,256]{1,0:T(8,128)(2,1)S(1)}, s32[16]{0:T(128)S(1)}) custom-call(s32[16]{0:T(128)S(1)} %bitcast.15, f32[16]{0:T(128)S(1)} %bitcast_convert_fusion.weight_ref, bf16[16,64,256]{2,1,0:T(8,128)(2,1)S(1)} %bitcast.10, s32[16,64,256]{2,1,0:T(8,128)S(1)} %bitcast.13), custom_call_target="tpu_custom_call" | custom-call | bytes 2097152 | tf_op jit(solution)/shard_map/partial_sums/pallas_call | solution.py:268
  5.8 0.0 copy-start.1
  5.8 5.1 %collective-permute-start.2 = (bf16[272,256]{1,0:T(8,128)(2,1)S(1)}, bf16[272,256]{1,0:T(8,128)(2,1)S(1)}, u32[]{:S(2)}, u32[]{:S(2)}) collective-permute-start(bf16[272,256]{1,0:T(8,128)(2,1)S(1)} %get-tuple-element.11.refs_0_.refs_1_), channel_id=1, source_target_pairs={{0,12},{4,0},{8,4},{12,8},{1,13},{5,1},{9,5},{13,9},{2,14},{6,2},{... | collective-permute-start | bytes 417800 | tf_op jit(solution)/shard_map/ppermute | solution.py:307
  10.9 0.0 collective-permute-start.1
  10.9 1.0 %collective-permute-start = (bf16[272,256]{1,0:T(8,128)(2,1)S(1)}, bf16[272,256]{1,0:T(8,128)(2,1)S(1)}, u32[]{:S(2)}, u32[]{:S(2)}) collective-permute-start(bf16[272,256]{1,0:T(8,128)(2,1)S(1)} %get-tuple-element.11.refs_0_.refs_1_), channel_id=1, source_target_pairs={{0,4},{4,8},{8,12},{12,0},{1,5},{5,9},{9,13},{13,1},{2,6},{6,10},{... | collective-permute-start | bytes 417800 | tf_op jit(solution)/shard_map/ppermute | solution.py:307
  11.9 0.1 pad_add_fusion.info_ref
  12.0 3.0 %collective-permute-done.2.refs_4_ = bf16[272,256]{1,0:T(8,128)(2,1)S(1)} collective-permute-done((bf16[272,256]{1,0:T(8,128)(2,1)S(1)}, bf16[272,256]{1,0:T(8,128)(2,1)S(1)}, u32[]{:S(2)}, u32[]{:S(2)}) %collective-permute-start.2) | collective-permute-done | bytes 139296 | tf_op jit(solution)/shard_map/ppermute | solution.py:307
  15.0 7.7 %collective-permute-done.1.refs_3_ = bf16[272,256]{1,0:T(8,128)(2,1)S(1)} collective-permute-done((bf16[272,256]{1,0:T(8,128)(2,1)S(1)}, bf16[272,256]{1,0:T(8,128)(2,1)S(1)}, u32[]{:S(2)}, u32[]{:S(2)}) %collective-permute-start.1) | collective-permute-done | bytes 139296 | tf_op jit(solution)/shard_map/ppermute | solution.py:307
  22.7 0.0 collective-permute-done.refs_2_
  22.7 0.0 copy-done.7
  22.7 1.4 %combine.1 = (bf16[2,64,256]{2,1,0:T(8,128)(2,1)S(1)}, bf16[2,16,256]{2,1,0:T(8,128)(2,1)S(1)}, bf16[64,256]{1,0:T(8,128)(2,1)}) custom-call(s32[2]{0:T(128)S(1)} %pad_add_fusion.info_ref, s32[4]{0:T(128)S(1)} %copy-done.7, bf16[272,256]{1,0:T(8,128)(2,1)S(1)} %get-tuple-element.11.refs_0_.refs_1_, bf16[272,256]{1,0:T(8,128)(2,1)S(1)} %get-tuple-element.11.refs_0_.refs_1_, ...), custom_call_target="tpu_custom_call" | custom-call | bytes 1048576 | tf_op jit(solution)/shard_map/combine/pallas_call | solution.py:268
  24.1 1.5 %collective-permute-start.3 = (bf16[2,16,256]{2,1,0:T(8,128)(2,1)S(1)}, bf16[2,16,256]{2,1,0:T(8,128)(2,1)S(1)}, u32[]{:S(2)}, u32[]{:S(2)}) collective-permute-start(bf16[2,16,256]{2,1,0:T(8,128)(2,1)S(1)} %get-tuple-element.15), channel_id=1, source_target_pairs={{0,2},{2,0},{1,3},{3,1},{4,6},{6,4},{5,7},{7,5},{8,10},{10,8},{9,1... | collective-permute-start | bytes 49160 | tf_op jit(solution)/shard_map/ppermute | solution.py:335
  25.6 0.0 copy-done.3
  25.6 0.0 copy-done.1
  25.6 0.7 %sorted_usable.1 = (bf16[2,128,1024]{2,1,0:T(8,128)(2,1)S(1)}, bf16[2,128,1024]{2,1,0:T(8,128)(2,1)S(1)}) custom-call(s32[16]{0:T(128)S(1)} %get-tuple-element.13.order_ref, bf16[16,64,256]{2,1,0:T(8,128)(2,1)S(1)} %bitcast.11, s32[16,64,256]{2,1,0:T(8,128)S(1)} %bitcast.14), custom_call_target="tpu_custom_call" | custom-call | bytes 3145728 | tf_op jit(solution)/shard_map/sorted_usable/pallas_call | solution.py:268
  26.4 1.5 %collective-permute-done.3.refs_0_ = bf16[2,16,256]{2,1,0:T(8,128)(2,1)S(1)} collective-permute-done((bf16[2,16,256]{2,1,0:T(8,128)(2,1)S(1)}, bf16[2,16,256]{2,1,0:T(8,128)(2,1)S(1)}, u32[]{:S(2)}, u32[]{:S(2)}) %collective-permute-start.3) | collective-permute-done | bytes 16416 | tf_op jit(solution)/shard_map/ppermute | solution.py:335
  27.9 2.4 %normal_equations.1 = (bf16[2,96,1024]{2,1,0:T(8,128)(2,1)S(1)}, f32[16,128]{1,0:T(8,128)S(1)}) custom-call(s32[2]{0:T(128)S(1)} %pad_add_fusion.info_ref, bf16[2,64,256]{2,1,0:T(8,128)(2,1)S(1)} %get-tuple-element.14.template_ref, bf16[2,16,256]{2,1,0:T(8,128)(2,1)S(1)} %collective-permute-done.3.refs_0_, bf16[2,192,80]{2,1,0:T(8,128)(2,1)S(1)} %copy-done.5, ...), custom_call_target="tpu_custom_call" | custom-call | bytes 2097152 | tf_op jit(solution)/shard_map/normal_equations/pallas_call | solution.py:268
  30.3 1.5 %collective-permute-start.4 = (f32[16,128]{1,0:T(8,128)S(1)}, f32[16,128]{1,0:T(8,128)S(1)}, u32[]{:S(2)}, u32[]{:S(2)}) collective-permute-start(f32[16,128]{1,0:T(8,128)S(1)} %get-tuple-element.18.refs_0_), channel_id=1, source_target_pairs={{0,2},{2,0},{1,3},{3,1},{4,6},{6,4},{5,7},{7,5},{8,10},{10,8},{9,1... | collective-permute-start | bytes 24584 | tf_op jit(solution)/shard_map/ppermute | solution.py:361
  31.8 2.2 %collective-permute-done.4.refs_1_ = f32[16,128]{1,0:T(8,128)S(1)} collective-permute-done((f32[16,128]{1,0:T(8,128)S(1)}, f32[16,128]{1,0:T(8,128)S(1)}, u32[]{:S(2)}, u32[]{:S(2)}) %collective-permute-start.4) | collective-permute-done | bytes 8224 | tf_op jit(solution)/shard_map/ppermute | solution.py:361
  33.9 2.7 %fit.1 = bf16[16,64,256]{2,1,0:T(8,128)(2,1)} custom-call(s32[16]{0:T(128)S(1)} %get-tuple-element.13.order_ref, f32[16,128]{1,0:T(8,128)S(1)} %get-tuple-element.18.refs_0_, f32[16,128]{1,0:T(8,128)S(1)} %collective-permute-done.4.refs_1_, bf16[2,96,1024]{2,1,0:T(8,128)(2,1)S(1)} %get-tuple-element.19.refs_2_, bf16[16,64,256]{2,1,0:T(8,128)(2,1)S(1)} %bitcast.12), custom_call_target="tpu_custom_call" | custom-call | bytes 2097152 | tf_op jit(solution)/shard_map/fit/pallas_call | solution.py:268
  (9 shorter events, 0.0 us)
Async XLA Ops:
  1.3 0.7 %copy-start.6 = (s32[16,1]{0,1:T(1,128)S(1)}, s32[16,1]{0,1:T(1,128)}, u32[]{:S(2)}) copy-start(s32[16,1]{0,1:T(1,128)} %param.10) | copy-start | bytes 196
  1.9 1.0 %copy-start = (bf16[1,16,64,256]{3,2,1,0:T(8,128)(2,1)S(1)}, bf16[1,16,64,256]{3,2,1,0:T(8,128)(2,1)}, u32[]{:S(2)}) copy-start(bf16[1,16,64,256]{3,2,1,0:T(8,128)(2,1)} %param.7) | copy-start | bytes 1572868
  3.0 1.2 %copy-start.2 = (s32[1,16,64,256]{3,2,1,0:T(8,128)S(1)}, s32[1,16,64,256]{3,2,1,0:T(8,128)}, u32[]{:S(2)}) copy-start(s32[1,16,64,256]{3,2,1,0:T(8,128)} %param.8) | copy-start | bytes 3145732
  4.2 18.5 %copy-start.7 = (s32[4]{0:T(128)S(1)}, s32[4]{0:T(128)}, u32[]{:S(2)}) copy-start(s32[4]{0:T(128)} %owner_ref.1) | copy-start | bytes 52
  4.2 21.4 %copy-start.3 = (s32[1,16,64,256]{3,2,1,0:T(8,128)S(1)}, s32[1,16,64,256]{3,2,1,0:T(8,128)}, u32[]{:S(2)}) copy-start(s32[1,16,64,256]{3,2,1,0:T(8,128)} %param.8) | copy-start | bytes 3145732
  5.8 19.8 %copy-start.1 = (bf16[1,16,64,256]{3,2,1,0:T(8,128)(2,1)S(1)}, bf16[1,16,64,256]{3,2,1,0:T(8,128)(2,1)}, u32[]{:S(2)}) copy-start(bf16[1,16,64,256]{3,2,1,0:T(8,128)(2,1)} %param.7) | copy-start | bytes 1572868
  5.8 9.2 %collective-permute-start.2 = (bf16[272,256]{1,0:T(8,128)(2,1)S(1)}, bf16[272,256]{1,0:T(8,128)(2,1)S(1)}, u32[]{:S(2)}, u32[]{:S(2)}) collective-permute-start(bf16[272,256]{1,0:T(8,128)(2,1)S(1)} %get-tuple-element.11.refs_0_.refs_1_), channel_id=1, source_target_pairs={{0,12},{4,0},{8,4},{12,8},{1,13},{5,1},{9,5},{13,9},{2,14},{6,2},{... | collective-permute-start | bytes 417800 | tf_op jit(solution)/shard_map/ppermute | solution.py:307
  10.9 11.8 %collective-permute-start.1 = (bf16[272,256]{1,0:T(8,128)(2,1)S(1)}, bf16[272,256]{1,0:T(8,128)(2,1)S(1)}, u32[]{:S(2)}, u32[]{:S(2)}) collective-permute-start(bf16[272,256]{1,0:T(8,128)(2,1)S(1)} %get-tuple-element.11.refs_0_.refs_1_), channel_id=1, source_target_pairs={{0,8},{4,12},{8,0},{12,4},{1,9},{5,13},{9,1},{13,5},{2,10},{6,14},... | collective-permute-start | bytes 417800 | tf_op jit(solution)/shard_map/ppermute | solution.py:307
  10.9 11.8 %collective-permute-start = (bf16[272,256]{1,0:T(8,128)(2,1)S(1)}, bf16[272,256]{1,0:T(8,128)(2,1)S(1)}, u32[]{:S(2)}, u32[]{:S(2)}) collective-permute-start(bf16[272,256]{1,0:T(8,128)(2,1)S(1)} %get-tuple-element.11.refs_0_.refs_1_), channel_id=1, source_target_pairs={{0,4},{4,8},{8,12},{12,0},{1,5},{5,9},{9,13},{13,1},{2,6},{6,10},{... | collective-permute-start | bytes 417800 | tf_op jit(solution)/shard_map/ppermute | solution.py:307
  24.1 3.7 %collective-permute-start.3 = (bf16[2,16,256]{2,1,0:T(8,128)(2,1)S(1)}, bf16[2,16,256]{2,1,0:T(8,128)(2,1)S(1)}, u32[]{:S(2)}, u32[]{:S(2)}) collective-permute-start(bf16[2,16,256]{2,1,0:T(8,128)(2,1)S(1)} %get-tuple-element.15), channel_id=1, source_target_pairs={{0,2},{2,0},{1,3},{3,1},{4,6},{6,4},{5,7},{7,5},{8,10},{10,8},{9,1... | collective-permute-start | bytes 49160 | tf_op jit(solution)/shard_map/ppermute | solution.py:335
  25.6 2.2 %copy-start.4 = (bf16[3,256,256]{2,1,0:T(8,128)(2,1)S(1)}, bf16[3,256,256]{2,1,0:T(8,128)(2,1)}, u32[]{:S(2)}) copy-start(bf16[3,256,256]{2,1,0:T(8,128)(2,1)} %constant.14.clone.refs_2_) | copy-start | bytes 1179652
  25.6 2.2 %copy-start.5 = (bf16[2,192,80]{2,1,0:T(8,128)(2,1)S(1)}, bf16[2,192,80]{2,1,0:T(8,128)(2,1)}, u32[]{:S(2)}) copy-start(bf16[2,192,80]{2,1,0:T(8,128)(2,1)} %constant.13.clone.refs_1_) | copy-start | bytes 184324
  30.3 3.7 %collective-permute-start.4 = (f32[16,128]{1,0:T(8,128)S(1)}, f32[16,128]{1,0:T(8,128)S(1)}, u32[]{:S(2)}, u32[]{:S(2)}) collective-permute-start(f32[16,128]{1,0:T(8,128)S(1)} %get-tuple-element.18.refs_0_), channel_id=1, source_target_pairs={{0,2},{2,0},{1,3},{3,1},{4,6},{6,4},{5,7},{7,5},{8,10},{10,8},{9,1... | collective-permute-start | bytes 24584 | tf_op jit(solution)/shard_map/ppermute | solution.py:361
where the time goes:
time: 36.8 us; the launch traced here: 36.6 us
  waiting for transfers between devices  14.4 us (39%)
  starting transfers between devices  9.11 us (25%)
  Pallas kernels  8.74 us (24%)
  local copies, waits for them, and re-layouts  2.94 us (8%)
  other arithmetic  0.73 us (2%)
  between operations  0.67 us (2%)
    ppermute x3, waiting for transfers between devices, body(): lax.ppermute(message, 'visit', [(i, (i + shift) % visits) for i in range(...  10.7 us
    pallas_call x5, Pallas kernels, call(): pl.pallas_call(kernel, out_shape=outs, in_specs=in_specs, out_specs=out_s...  8.74 us
    ppermute x3, starting transfers between devices, body(): lax.ppermute(message, 'visit', [(i, (i + shift) % visits) for i in range(...  6.11 us
    unnamed x16, local copies, waits for them, and re-layouts  2.94 us
    ppermute x1, waiting for transfers between devices, body(): totals = [sums, lax.ppermute(sums, 'strip', [(0, 1), (1, 0)])]  2.16 us
    ppermute x1, starting transfers between devices, body(): totals = [sums, lax.ppermute(sums, 'strip', [(0, 1), (1, 0)])]  1.51 us
    ppermute x1, waiting for transfers between devices, body(): halos = [lax.ppermute(edge, 'strip', [(0, 1), (1, 0)])]  1.51 us
    ppermute x1, starting transfers between devices, body(): halos = [lax.ppermute(edge, 'strip', [(0, 1), (1, 0)])]  1.49 us
  transfers between devices with their start and end apart: 5, of which 4 were waited for; matrix products, arithmetic and copies ran while one was open for 0% of the time, Pallas kernels for 2%

commit v1 on v0

v1 whole, which is shorter than its diff:
```python
import functools

import jax
import jax.numpy as jnp
import ml_dtypes
import numpy as np
from jax import lax
from jax.experimental import pallas as pl
from jax.experimental.pallas import tpu as pltpu
from jax.sharding import PartitionSpec as P

BASES = 6
HALF = 9
TILE = 16
basis_rows = (0, 0, 1, 0, 2, 1)
basis_cols = (0, 1, 0, 2, 0, 1)
VMEM_LIMIT = 48 * 1024 * 1024
FETCH_LIMIT = 56 * 1024 * 1024

VMEM = pl.BlockSpec(memory_space=pltpu.VMEM)
SMEM = pl.BlockSpec(memory_space=pltpu.SMEM)
HBM = pl.BlockSpec(memory_space=pltpu.HBM)


def tap_rows():
    offsets = np.arange(2 * HALF + 1).astype(np.float64) - HALF
    gaussian = np.exp(-offsets * offsets / 18.0)
    squared = gaussian * gaussian
    centre = np.sum(offsets * offsets * squared) / np.sum(squared)
    table = np.stack([gaussian, offsets * gaussian, (offsets * offsets - centre) * gaussian])
    table = table / np.sqrt(np.sum(table * table, axis=1, keepdims=True))
    return table.astype(ml_dtypes.bfloat16)


def across_matrices(cols):
    taps = tap_rows()
    distance = np.arange(cols)[:, None] - np.arange(cols)[None, :] + HALF
    inside = (distance >= 0) & (distance <= 2 * HALF)
    return np.where(inside[None], taps[:, np.clip(distance, 0, 2 * HALF)], 0).astype(ml_dtypes.bfloat16)


def vertical_matrix(rows, sources):
    taps = tap_rows()
    distance = np.asarray(sources)[None, :] - np.arange(rows)[:, None] + HALF
    inside = (distance >= 0) & (distance <= 2 * HALF)
    table = np.where(inside[None], taps[:, np.clip(distance, 0, 2 * HALF)], 0)
    return table.reshape(3 * rows, len(sources)).astype(ml_dtypes.bfloat16)


def unusable(mask):
    return jnp.bitwise_and(mask, 3) == 3


def piece_order(ids_ref, order_ref):
    pieces = order_ref.shape[0]
    ids = [ids_ref[j] for j in range(pieces)]
    for j in range(pieces):
        place = jnp.int32(0)
        for i in range(pieces):
            if i < j:
                place = place + (ids[i] <= ids[j]).astype(jnp.int32)
            elif i > j:
                place = place + (ids[i] < ids[j]).astype(jnp.int32)
        order_ref[place] = j


def piece_weights(weight_ref, splat_ref):
    weights = weight_ref[...].astype(jnp.float32)
    for j in range(splat_ref.shape[0]):
        splat_ref[j] = weights[0, j]


def windows(half, halves):
    if not halves:
        return 0, 0
    strip = lax.axis_index("strip")
    return pl.multiple_of((1 - strip) * half, TILE), pl.multiple_of(strip * half, TILE)


def put_sums(slots, cap, order_ref, weight_ref, image_of, mask_of, message_ref, base):
    cols = message_ref.shape[1]
    for slot in range(slots):
        numerator = jnp.zeros((TILE, cols), jnp.float32)
        denominator = jnp.zeros((TILE, cols), jnp.float32)
        for k in range(cap):
            j = order_ref[slot * cap + k]
            weight = jnp.where(unusable(mask_of(j)), 0.0, weight_ref[j])
            denominator = denominator + weight
            numerator = numerator + weight * image_of(j).astype(jnp.float32)
        at = base + slot * 2 * TILE
        message_ref[at : at + TILE, :] = numerator.astype(jnp.bfloat16)
        message_ref[at + TILE : at + 2 * TILE, :] = denominator.astype(jnp.bfloat16)


def first_kernel(slots, cap, half, halves, ids_hbm, weight_hbm, image_hbm, mask_hbm, message_hbm, *refs):
    message_ref, order_ref, splat_ref, ids_ref, weight_ref, image_ref, mask_ref, small_sem, sem, out_sem = refs
    cols = image_ref.shape[2]
    tiles = half // TILE
    first = windows(half, halves)[0]
    small = [
        pltpu.make_async_copy(ids_hbm, ids_ref, small_sem.at[0]),
        pltpu.make_async_copy(weight_hbm, weight_ref, small_sem.at[1]),
    ]
    large = []
    for g in range(tiles):
        source = pl.ds(first + g * TILE, TILE)
        here = slice(g * TILE, (g + 1) * TILE)
        large.append(
            (
                pltpu.make_async_copy(mask_hbm.at[:, source, :], mask_ref.at[:, here, :], sem.at[g, 0]),
                pltpu.make_async_copy(image_hbm.at[:, source, :], image_ref.at[:, here, :], sem.at[g, 1]),
            )
        )
    for copy in small:
        copy.start()
    for pair in large:
        for copy in pair:
            copy.start()
    for copy in small:
        copy.wait()
    piece_order(ids_ref, order_ref)
    piece_weights(weight_ref, splat_ref)
    label_rows = message_ref.shape[0] - tiles * slots * 2 * TILE
    line = lax.broadcasted_iota(jnp.int32, (label_rows, cols), 0)
    labels = jnp.zeros((label_rows, cols), jnp.float32)
    for slot in range(slots):
        labels = jnp.where(line == slot, ids_ref[order_ref[slot * cap]].astype(jnp.float32), labels)
    message_ref[:label_rows, :] = labels.astype(jnp.bfloat16)
    done, copies = 0, []
    for g in range(tiles):
        for copy in large[g]:
            copy.wait()
        here = slice(g * TILE, (g + 1) * TILE)
        base = label_rows + g * slots * 2 * TILE
        put_sums(
            slots,
            cap,
            order_ref,
            splat_ref,
            lambda j, here=here: image_ref[j, here, :],
            lambda j, here=here: mask_ref[j, here, :],
            message_ref,
            base,
        )
        ready = pl.ds(done, base + slots * 2 * TILE - done)
        copies.append(pltpu.make_async_copy(message_ref.at[ready, :], message_hbm.at[ready, :], out_sem.at[g]))
        copies[-1].start()
        done = base + slots * 2 * TILE
    for copy in copies:
        copy.wait()


def second_kernel(slots, cap, half, ids_ref, weight_ref, image_ref, mask_ref, message_ref, order_ref, splat_ref):
    first = windows(half, True)[1]
    piece_order(ids_ref, order_ref)
    piece_weights(weight_ref, splat_ref)
    for g in range(half // TILE):
        here = pl.ds(first + g * TILE, TILE)
        put_sums(
            slots,
            cap,
            order_ref,
            splat_ref,
            lambda j, here=here: image_ref[j, here, :],
            lambda j, here=here: mask_ref[j, here, :],
            message_ref,
            g * slots * 2 * TILE,
        )


def sort_kernel(slots, cap, ids_ref, image_ref, mask_ref, usable_ref, masked_ref, order_ref):
    rows, cols = image_ref.shape[1:]
    piece_order(ids_ref, order_ref)
    for slot in range(slots):
        for k in range(cap):
            j = order_ref[slot * cap + k]
            for g in range(rows // TILE):
                lines = slice(g * TILE, (g + 1) * TILE)
                usable = jnp.where(unusable(mask_ref[j, lines, :]), 0.0, 1.0).astype(jnp.bfloat16)
                at = (slot, slice(k * TILE, (k + 1) * TILE), slice(g * cols, (g + 1) * cols))
                usable_ref[at] = usable
                masked_ref[at] = usable * image_ref[j, lines, :]


def owned_patch(owner_ref):
    visit = lax.axis_index("visit")
    mine = jnp.int32(0)
    for p in range(owner_ref.shape[0]):
        mine = jnp.where(owner_ref[p] == visit, p, mine)
    return mine.astype(jnp.float32)


def picks(labels, own_labels, mine, slots, slot):
    label = labels[slot : slot + 1, :]
    hits = [label == own_labels[t : t + 1, :] for t in range(slots)] + [label == mine]
    return [hit.astype(jnp.float32) for hit in hits]


def quotient(numerator, denominator):
    return (numerator / jnp.maximum(denominator, 1.0)).astype(jnp.bfloat16)


def combine(slots, rows, base, mine, labels, sources, put):
    cols = sources[0].shape[1]
    labels = [value.astype(jnp.float32) for value in labels]
    hits = [[picks(label, labels[0], mine, slots, slot) for slot in range(slots)] for label in labels]
    for first in range(0, rows, TILE):
        sums = [[jnp.zeros((TILE, cols), jnp.float32) for _ in range(2)] for _ in range(slots + 1)]
        for d, ref in enumerate(sources):
            for slot in range(slots):
                for kind in range(2):
                    at = base + first * slots * 2 + (slot * 2 + kind) * TILE
                    value = ref[at : at + TILE, :].astype(jnp.float32)
                    for t in range(slots + 1):
                        if d == 0 and t < slots:
                            if t == slot:
                                sums[t][kind] = sums[t][kind] + value
                        else:
                            sums[t][kind] = sums[t][kind] + hits[d][slot][t] * value
        for t in range(slots + 1):
            put(t, first, quotient(*sums[t]))


def border_kernel(slots, count, rows, owner_ref, *refs):
    sources, (template_ref, coadd_ref, edge_ref) = refs[:count], refs[count:]
    base = sources[0].shape[0] - rows * slots * 2
    labels = [ref[:base, :] for ref in sources]

    def put(t, first, value):
        if t < slots:
            template_ref[t, first : first + TILE, :] = value
        else:
            coadd_ref[first : first + TILE, :] = value

    combine(slots, rows, base, owned_patch(owner_ref), labels, sources, put)
    at = pl.multiple_of((1 - lax.axis_index("strip")) * (rows - TILE), TILE)
    edge_ref[...] = template_ref[:, pl.ds(at, TILE), :]


def gathered_kernel(slots, owner_ref, stacked_ref, template_ref, coadd_ref, edge_ref, total_ref):
    rows, cols = coadd_ref.shape
    base = stacked_ref.shape[1] - rows * slots * 2
    mine = owned_patch(owner_ref)
    own_labels = stacked_ref[lax.axis_index("visit"), :base, :].astype(jnp.float32)
    total_ref[...] = jnp.zeros_like(total_ref)

    def add_source(d, carry):
        labels = stacked_ref[d, :base, :].astype(jnp.float32)
        for slot in range(slots):
            pick = picks(labels, own_labels, mine, slots, slot)
            for kind in range(2):
                for first in range(0, rows, TILE):
                    at = base + first * slots * 2 + (slot * 2 + kind) * TILE
                    value = stacked_ref[d, at : at + TILE, :].astype(jnp.float32)
                    for t in range(slots + 1):
                        total_ref[t, kind, first : first + TILE, :] += pick[t] * value
        return carry

    lax.fori_loop(0, stacked_ref.shape[0], add_source, 0)
    for t in range(slots):
        template_ref[t] = quotient(total_ref[t, 0], total_ref[t, 1])
    coadd_ref[...] = quotient(total_ref[slots, 0], total_ref[slots, 1])
    edge_ref[:, :TILE, :] = template_ref[:, :TILE, :]
    edge_ref[:, TILE:, :] = template_ref[:, rows - TILE :, :]


def halves_kernel(slots, cap, count, rows, owner_ref, *refs):
    firsts, seconds, refs = refs[:count], refs[count : 2 * count], refs[2 * count :]
    template_ref, halo_ref, coadd_ref, vertical_ref, across_ref, usable_ref, masked_ref = refs[:7]
    basis_ref, sums_ref, whole_ref, second_ref, smooth_ref, left_ref = refs[7:]
    labels = [ref[: ref.shape[0] - rows * slots * 2, :] for ref in firsts]
    early, late = windows(rows, True)
    whole_ref[pl.ds(early, rows), :] = coadd_ref[...]

    def put(t, first, value):
        if t < slots:
            second_ref[t, first : first + TILE, :] = value
        else:
            whole_ref[pl.ds(late + first, TILE), :] = value

    combine(slots, rows, 0, owned_patch(owner_ref), labels, seconds, put)
    normal_equations(
        slots,
        cap,
        [template_ref, second_ref, halo_ref],
        vertical_ref[lax.axis_index("strip")],
        across_ref,
        usable_ref,
        masked_ref,
        basis_ref,
        sums_ref,
        smooth_ref,
        left_ref,
    )


def normal_kernel(slots, cap, template_ref, below_ref, above_ref, vertical_ref, *refs):
    normal_equations(slots, cap, [template_ref, below_ref, above_ref], vertical_ref[0], *refs)


def normal_equations(
    slots, cap, parts, vertical, across_ref, usable_ref, masked_ref, basis_ref, sums_ref, smooth_ref, left_ref
):
    rows, cols = smooth_ref.shape[2:]
    tiles = rows // TILE
    for slot in range(slots):
        extended = jnp.concatenate([ref[slot] for ref in parts], axis=0)
        smooth = jnp.dot(vertical, extended, preferred_element_type=jnp.float32)
        for k in range(3):
            smooth_ref[k, slot] = smooth[k * rows : (k + 1) * rows].astype(jnp.bfloat16)
    for c in range(3):
        users = [a for a in range(BASES) if basis_cols[a] == c]
        for slot in range(slots):
            stacked = jnp.concatenate([smooth_ref[basis_rows[a], slot] for a in users], axis=0)
            planes = jnp.dot(stacked, across_ref[c], preferred_element_type=jnp.float32).astype(jnp.bfloat16)
            for n, a in enumerate(users):
                for g in range(tiles):
                    at = n * rows + g * TILE
                    basis_ref[slot, a * TILE : (a + 1) * TILE, g * cols : (g + 1) * cols] = planes[at : at + TILE]
    group = cap * TILE
    height = BASES * group + group
    for slot in range(slots):
        for a in range(BASES):
            plane = basis_ref[slot, a * TILE : (a + 1) * TILE, :]
            for k in range(cap):
                at = a * group + k * TILE
                left_ref[at : at + TILE, :] = plane * usable_ref[slot, k * TILE : (k + 1) * TILE, :]
        left_ref[BASES * group :, :] = masked_ref[slot]
        product = lax.dot_general(
            left_ref[...], basis_ref[slot], (((1,), (1,)), ((), ())), preferred_element_type=jnp.float32
        )
        width = product.shape[1]
        line = lax.broadcasted_iota(jnp.int32, (TILE, width), 0)
        lane = lax.broadcasted_iota(jnp.int32, (TILE, width), 1)
        same = line == lane % TILE
        product = jnp.where(same[None], product.reshape(height // TILE, TILE, width), 0.0)
        product = jnp.sum(product, axis=1)
        product = jnp.concatenate([product, jnp.zeros((height // TILE, 128 - width), jnp.float32)], axis=1)
        for step in (1, 2, 4, 8):
            product = product + pltpu.roll(product, 128 - step, 1)
        lanes = lax.broadcasted_iota(jnp.int32, product.shape, 1)
        product = jnp.where(lanes % TILE == 0, product, 0.0)
        packed = product[:cap]
        for a in range(1, BASES + 1):
            packed = packed + pltpu.roll(product[a * cap : (a + 1) * cap], a, 1)
        sums_ref[slot * cap : (slot + 1) * cap, :] = packed


def fit_kernel(slots, cap, order_ref, *refs):
    sums_refs, (basis_ref, image_ref, difference_hbm, difference_ref, sem) = refs[:-5], refs[-5:]
    rows, cols = image_ref.shape[1:]
    tiles = rows // TILE
    total = sums_refs[0][...]
    for ref in sums_refs[1:]:
        total = total + ref[...]
    pieces = total.shape[0]
    lanes = lax.broadcasted_iota(jnp.int32, (pieces, 128), 1)
    starts = lanes % TILE == 0
    table = []
    for c in range(BASES + 1):
        line = total if c == 0 else pltpu.roll(total, 128 - c, 1)
        line = jnp.where(starts, line, 0.0)
        if c < BASES:
            line = line + jnp.where(lanes == c * TILE, 1.0, 0.0)
        table.append(line)
    for k in range(BASES):
        at = k * TILE
        pivot = table[k]
        inverse = 1.0 / pivot[:, at : at + 1]
        for c in range(k + 1, BASES + 1):
            ratio = table[c][:, at : at + 1] * inverse
            table[c] = jnp.where(lanes == at, ratio, table[c] - pivot * ratio)
    spread = table[BASES]
    for step in (1, 2, 4, 8):
        spread = spread + pltpu.roll(spread, step, 1)
    line = lax.broadcasted_iota(jnp.int32, (TILE, 128), 0)
    lane = lax.broadcasted_iota(jnp.int32, (TILE, 128), 1)
    same = (line == lane % TILE) & (lane < BASES * TILE)
    copies = []
    for slot in range(slots):
        blocks = [
            jnp.where(same, spread[slot * cap + k : slot * cap + k + 1, :], 0.0) for k in range(cap)
        ]
        exact = jnp.concatenate(blocks, axis=0)[:, : BASES * TILE]
        high = exact.astype(jnp.bfloat16)
        low = (exact - high.astype(jnp.float32)).astype(jnp.bfloat16)
        basis = basis_ref[slot]
        fitted = jnp.dot(high, basis, preferred_element_type=jnp.float32) + jnp.dot(
            low, basis, preferred_element_type=jnp.float32
        )
        for k in range(cap):
            j = order_ref[slot * cap + k]
            place = slot * cap + k
            for g in range(tiles):
                part = fitted[k * TILE : (k + 1) * TILE, g * cols : (g + 1) * cols]
                image = image_ref[j, g * TILE : (g + 1) * TILE, :].astype(jnp.float32)
                difference_ref[place, g * TILE : (g + 1) * TILE, :] = (image - part).astype(jnp.bfloat16)
            copy = pltpu.make_async_copy(difference_ref.at[place], difference_hbm.at[j], sem.at[place])
            copy.start()
            copies.append(copy)
    for copy in copies:
        copy.wait()


def call(kernel, name, outs, in_specs, out_specs, args, scratch=(), flops=0, size=0, limit=VMEM_LIMIT):
    return pl.pallas_call(
        kernel,
        out_shape=outs,
        in_specs=in_specs,
        out_specs=out_specs,
        scratch_shapes=list(scratch),
        name=name,
        compiler_params=pltpu.CompilerParams(vmem_limit_bytes=limit),
        cost_estimate=pl.CostEstimate(flops=flops, bytes_accessed=size, transcendentals=0),
    )(*args)


def body(images, mask_bits, visit_weight, intersection, patch_owner):
    visits = lax.axis_size("visit")
    strips = lax.axis_size("strip")
    _, pieces, rows, cols = images.shape
    slots = visits // 2
    cap = pieces // slots
    tiles = rows // TILE
    shape = jax.ShapeDtypeStruct
    bf16, f32 = jnp.bfloat16, jnp.float32
    image = images[0]
    mask = mask_bits[0]
    halves = strips == 2 and visits <= 4
    half = rows // 2 if halves else rows
    ids = intersection[:, 0]
    label_rows = -(-slots // TILE) * TILE
    message_shape = (label_rows + slots * 2 * half, cols)

    message = call(
        functools.partial(first_kernel, slots, cap, half, halves),
        "first_sums",
        shape(message_shape, bf16),
        [HBM] * 4,
        HBM,
        (ids, visit_weight, image, mask),
        scratch=[
            pltpu.VMEM(message_shape, bf16),
            pltpu.SMEM((pieces,), jnp.int32),
            pltpu.SMEM((pieces,), f32),
            pltpu.SMEM((pieces,), jnp.int32),
            pltpu.VMEM((1, pieces), bf16),
            pltpu.VMEM((pieces, half, cols), bf16),
            pltpu.VMEM((pieces, half, cols), jnp.int32),
            pltpu.SemaphoreType.DMA((2,)),
            pltpu.SemaphoreType.DMA((half // TILE, 2)),
            pltpu.SemaphoreType.DMA((half // TILE,)),
        ],
        size=2 << 20,
        limit=FETCH_LIMIT,
    )

    def everyone(value):
        others = [
            lax.ppermute(value, "visit", [(i, (i + shift) % visits) for i in range(visits)])
            for shift in range(1, visits)
        ]
        return [value] + others

    sorted_shape = shape((slots, cap * TILE, tiles * cols), bf16)
    if halves:
        firsts = everyone(message)
        second = call(
            functools.partial(second_kernel, slots, cap, half),
            "second_sums",
            shape((slots * 2 * half, cols), bf16),
            [SMEM] + [VMEM] * 3,
            VMEM,
            (ids, visit_weight, image, mask),
            scratch=[pltpu.SMEM((pieces,), jnp.int32), pltpu.SMEM((pieces,), f32)],
            size=1 << 20,
        )
        seconds = everyone(second)
    usable, masked, order = call(
        functools.partial(sort_kernel, slots, cap),
        "sorted_usable",
        (sorted_shape, sorted_shape, shape((pieces,), jnp.int32)),
        [SMEM, VMEM, VMEM],
        (VMEM, VMEM, SMEM),
        (ids, image, mask),
        size=3 << 20,
    )
    normal_outs = (shape((slots, BASES * TILE, tiles * cols), bf16), shape((pieces, 128), f32))
    normal_scratch = [
        pltpu.VMEM((3, slots, rows, cols), bf16),
        pltpu.VMEM(((BASES + 1) * cap * TILE, tiles * cols), bf16),
    ]
    across = jnp.asarray(across_matrices(cols))
    if halves:
        template, coadd, edge = call(
            functools.partial(border_kernel, slots, visits, half),
            "border",
            (shape((slots, half, cols), bf16), shape((half, cols), bf16), shape((slots, TILE, cols), bf16)),
            [SMEM] + [VMEM] * visits,
            (VMEM,) * 3,
            (patch_owner, *firsts),
            size=1 << 20,
        )
        halo = lax.ppermute(edge, "strip", [(0, 1), (1, 0)])
        low, high = list(range(half)), list(range(half, rows))
        vertical = np.stack(
            [
                vertical_matrix(rows, high + low + list(range(rows, rows + TILE))),
                vertical_matrix(rows, low + high + list(range(-TILE, 0))),
            ]
        )
        basis, sums, coadd = call(
            functools.partial(halves_kernel, slots, cap, visits, half),
            "normal_equations",
            (*normal_outs, shape((rows, cols), bf16)),
            [SMEM] + [VMEM] * (2 * visits + 7),
            (VMEM,) * 3,
            (
                patch_owner,
                *firsts,
                *seconds,
                template,
                halo,
                coadd,
                jnp.asarray(vertical),
                across,
                usable,
                masked,
            ),
            scratch=[pltpu.VMEM((slots, half, cols), bf16)] + normal_scratch,
            size=2 << 20,
        )
        totals = [sums, lax.ppermute(sums, "strip", [(0, 1), (1, 0)])]
    else:
        template, coadd, edge = call(
            functools.partial(gathered_kernel, slots),
            "combine",
            (shape((slots, rows, cols), bf16), shape((rows, cols), bf16), shape((slots, 2 * TILE, cols), bf16)),
            [SMEM, VMEM],
            (VMEM,) * 3,
            (patch_owner, lax.all_gather(message, "visit")),
            scratch=[pltpu.VMEM((slots + 1, 2, rows, cols), f32)],
            size=1 << 20,
        )
        below = lax.ppermute(edge[:, TILE:], "strip", [(i, i + 1) for i in range(strips - 1)])
        above = lax.ppermute(edge[:, :TILE], "strip", [(i + 1, i) for i in range(strips - 1)])
        around = list(range(rows)) + list(range(-TILE, 0)) + list(range(rows, rows + TILE))
        basis, sums = call(
            functools.partial(normal_kernel, slots, cap),
            "normal_equations",
            normal_outs,
            [VMEM] * 7,
            (VMEM, VMEM),
            (template, below, above, jnp.asarray(vertical_matrix(rows, around)[None]), across, usable, masked),
            scratch=normal_scratch,
            size=2 << 20,
        )
        totals = [lax.psum(sums, "strip")]
    difference = call(
        functools.partial(fit_kernel, slots, cap),
        "fit",
        shape((pieces, rows, cols), bf16),
        [SMEM] + [VMEM] * (len(totals) + 2),
        HBM,
        (order, *totals, basis, image),
        scratch=[pltpu.VMEM((pieces, rows, cols), bf16), pltpu.SemaphoreType.DMA((pieces,))],
        size=2 << 20,
    )
    return (coadd[None, None], difference[None])


def solution(mesh):
    in_specs = (
        P("band", ("groups", "visit"), "strip", None),
        P("band", ("groups", "visit"), "strip", None),
        P("band", ("groups", "visit")),
        P(("groups", "visit"), None),
        P("groups"),
    )
    out_specs = (
        P("band", ("groups", "visit"), "strip", None),
        P("band", ("groups", "visit"), "strip", None),
    )
    return jax.shard_map(body, mesh=mesh, in_specs=in_specs, out_specs=out_specs, check_vma=False)
```

time: 36.8 us -> 30.5 us (0.83)
  the two profiles are of different devices: /device:TPU:0 before, /device:TPU:16 now
where the time goes in v1:
time: 30.5 us; the launch traced here: 30.3 us
  starting transfers between devices  10.9 us (36%)
  Pallas kernels  10.8 us (35%)
  waiting for transfers between devices  7.78 us (26%)
  between operations  0.77 us (3%)
    pallas_call x6, Pallas kernels, call(): pl.pallas_call(kernel, out_shape=outs, in_specs=in_specs, out_specs=out_s...  10.8 us
    ppermute x6, starting transfers between devices, everyone(): lax.ppermute(value, 'visit', [(i, (i + shift) % visits) for i in range(vi...  7.86 us
    ppermute x6, waiting for transfers between devices, everyone(): lax.ppermute(value, 'visit', [(i, (i + shift) % visits) for i in range(vi...  4.88 us
    ppermute x1, waiting for transfers between devices, body(): totals = [sums, lax.ppermute(sums, 'strip', [(0, 1), (1, 0)])]  2.16 us
    ppermute x1, starting transfers between devices, body(): halo = lax.ppermute(edge, 'strip', [(0, 1), (1, 0)])  1.56 us
    ppermute x1, starting transfers between devices, body(): totals = [sums, lax.ppermute(sums, 'strip', [(0, 1), (1, 0)])]  1.49 us
    ppermute x1, waiting for transfers between devices, body(): halo = lax.ppermute(edge, 'strip', [(0, 1), (1, 0)])  0.75 us
  transfers between devices with their start and end apart: 8, of which 3 were waited for; matrix products, arithmetic and copies ran while one was open for 0% of the time, Pallas kernels for 10%

profile of v1, /device:TPU:16, one launch (start us, length us, event | category | flops | bytes accessed | tf_op | source)
XLA Modules:
  0.0 30.3 jit_solution(14108311213801317816)
XLA Ops:
  0.7 2.0 %first_sums.1.refs_0_ = bf16[144,256]{1,0:T(8,128)(2,1)} custom-call(s32[16]{0:T(128)} %bitcast.12, bf16[1,16]{1,0:T(2,128)(2,1)} %weight_ref.1, bf16[16,64,256]{2,1,0:T(8,128)(2,1)} %bitcast.8, s32[16,64,256]{2,1,0:T(8,128)} %bitcast.5), custom_call_target="tpu_custom_call" | custom-call | bytes 2097152 | tf_op jit(solution)/shard_map/first_sums/pallas_call | solution.py:406
  2.7 0.0 copy-start.2
  2.7 0.0 copy-start.7
  2.7 0.5 %collective-permute-start.2 = (bf16[144,256]{1,0:T(8,128)(2,1)}, bf16[144,256]{1,0:T(8,128)(2,1)S(1)}, u32[]{:S(2)}, u32[]{:S(2)}) collective-permute-start(bf16[144,256]{1,0:T(8,128)(2,1)} %first_sums.1.refs_0_), channel_id=1, source_target_pairs={{0,12},{4,0},{8,4},{12,8},{1,13},{5,1},{9,5},{13,9},{2,14},{6,2},{... | collective-permute-start | bytes 221192 | tf_op jit(solution)/shard_map/ppermute | solution.py:460
  3.2 3.5 %collective-permute-start.1 = (bf16[144,256]{1,0:T(8,128)(2,1)}, bf16[144,256]{1,0:T(8,128)(2,1)S(1)}, u32[]{:S(2)}, u32[]{:S(2)}) collective-permute-start(bf16[144,256]{1,0:T(8,128)(2,1)} %first_sums.1.refs_0_), channel_id=1, source_target_pairs={{0,8},{4,12},{8,0},{12,4},{1,9},{5,13},{9,1},{13,5},{2,10},{6,14},... | collective-permute-start | bytes 221192 | tf_op jit(solution)/shard_map/ppermute | solution.py:460
  6.7 0.0 collective-permute-start
  6.7 1.0 %second_sums.1.refs_4_ = bf16[128,256]{1,0:T(8,128)(2,1)S(1)} custom-call(s32[16]{0:T(128)S(1)} %bitcast.13, bf16[1,16]{1,0:T(2,128)(2,1)S(1)} %copy-done.6, bf16[16,64,256]{2,1,0:T(8,128)(2,1)S(1)} %bitcast.9, s32[16,64,256]{2,1,0:T(8,128)S(1)} %bitcast.6), custom_call_target="tpu_custom_call" | custom-call | bytes 1048576 | tf_op jit(solution)/shard_map/second_sums/pallas_call | solution.py:406
  7.7 2.1 %collective-permute-start.5 = (bf16[128,256]{1,0:T(8,128)(2,1)S(1)}, bf16[128,256]{1,0:T(8,128)(2,1)S(1)}, u32[]{:S(2)}, u32[]{:S(2)}) collective-permute-start(bf16[128,256]{1,0:T(8,128)(2,1)S(1)} %second_sums.1.refs_4_), channel_id=1, source_target_pairs={{0,12},{4,0},{8,4},{12,8},{1,13},{5,1},{9,5},{13,9},{2,14},{6,2},{... | collective-permute-start | bytes 196616 | tf_op jit(solution)/shard_map/ppermute | solution.py:460
  9.8 1.8 %collective-permute-start.4 = (bf16[128,256]{1,0:T(8,128)(2,1)S(1)}, bf16[128,256]{1,0:T(8,128)(2,1)S(1)}, u32[]{:S(2)}, u32[]{:S(2)}) collective-permute-start(bf16[128,256]{1,0:T(8,128)(2,1)S(1)} %second_sums.1.refs_4_), channel_id=1, source_target_pairs={{0,8},{4,12},{8,0},{12,4},{1,9},{5,13},{9,1},{13,5},{2,10},{6,14},... | collective-permute-start | bytes 196616 | tf_op jit(solution)/shard_map/ppermute | solution.py:460
  11.6 0.0 collective-permute-done.2.refs_3_
  11.6 0.0 collective-permute-start.3
  11.6 0.0 collective-permute-done.1.refs_2_
  11.6 4.9 %collective-permute-done.refs_1_ = bf16[144,256]{1,0:T(8,128)(2,1)S(1)} collective-permute-done((bf16[144,256]{1,0:T(8,128)(2,1)}, bf16[144,256]{1,0:T(8,128)(2,1)S(1)}, u32[]{:S(2)}, u32[]{:S(2)}) %collective-permute-start) | collective-permute-done | bytes 73760 | tf_op jit(solution)/shard_map/ppermute | solution.py:460
  16.5 0.7 %border.1 = (bf16[2,32,256]{2,1,0:T(8,128)(2,1)S(1)}, bf16[32,256]{1,0:T(8,128)(2,1)S(1)}, bf16[2,16,256]{2,1,0:T(8,128)(2,1)S(1)}) custom-call(s32[4]{0:T(128)S(1)} %copy-done.7, bf16[144,256]{1,0:T(8,128)(2,1)S(1)} %copy-done.2, bf16[144,256]{1,0:T(8,128)(2,1)S(1)} %collective-permute-done.refs_1_, bf16[144,256]{1,0:T(8,128)(2,1)S(1)} %collective-permute-done.1.refs_2_, ...), custom_call_target="tpu_custom_call" | custom-call | bytes 1048576 | tf_op jit(solution)/shard_map/border/pallas_call | solution.py:406
  17.2 0.0 copy-start.3
  17.2 0.0 copy-start.4
  17.2 1.6 %collective-permute-start.6 = (bf16[2,16,256]{2,1,0:T(8,128)(2,1)S(1)}, bf16[2,16,256]{2,1,0:T(8,128)(2,1)S(1)}, u32[]{:S(2)}, u32[]{:S(2)}) collective-permute-start(bf16[2,16,256]{2,1,0:T(8,128)(2,1)S(1)} %get-tuple-element.12), channel_id=1, source_target_pairs={{0,2},{2,0},{1,3},{3,1},{4,6},{6,4},{5,7},{7,5},{8,10},{10,8},{9,1... | collective-permute-start | bytes 49160 | tf_op jit(solution)/shard_map/ppermute | solution.py:504
  18.7 1.5 %sorted_usable.1 = (bf16[2,128,1024]{2,1,0:T(8,128)(2,1)S(1)}, bf16[2,128,1024]{2,1,0:T(8,128)(2,1)S(1)}, s32[16]{0:T(128)S(1)}) custom-call(s32[16]{0:T(128)S(1)} %bitcast.14, bf16[16,64,256]{2,1,0:T(8,128)(2,1)S(1)} %bitcast.10, s32[16,64,256]{2,1,0:T(8,128)S(1)} %bitcast.7), custom_call_target="tpu_custom_call" | custom-call | bytes 3145728 | tf_op jit(solution)/shard_map/sorted_usable/pallas_call | solution.py:406
  20.2 0.0 collective-permute-done.5.refs_7_
  20.2 0.7 %collective-permute-done.6.refs_9_ = bf16[2,16,256]{2,1,0:T(8,128)(2,1)S(1)} collective-permute-done((bf16[2,16,256]{2,1,0:T(8,128)(2,1)S(1)}, bf16[2,16,256]{2,1,0:T(8,128)(2,1)S(1)}, u32[]{:S(2)}, u32[]{:S(2)}) %collective-permute-start.6) | collective-permute-done | bytes 16416 | tf_op jit(solution)/shard_map/ppermute | solution.py:504
  21.0 3.0 %normal_equations.1 = (bf16[2,96,1024]{2,1,0:T(8,128)(2,1)S(1)}, f32[16,128]{1,0:T(8,128)S(1)}, bf16[64,256]{1,0:T(8,128)(2,1)}) custom-call(s32[4]{0:T(128)S(1)} %copy-done.7, bf16[144,256]{1,0:T(8,128)(2,1)S(1)} %copy-done.2, bf16[144,256]{1,0:T(8,128)(2,1)S(1)} %collective-permute-done.refs_1_, bf16[144,256]{1,0:T(8,128)(2,1)S(1)} %collective-permute-done.1.refs_2_, ...), custom_call_target="tpu_custom_call" | custom-call | bytes 2097152 | tf_op jit(solution)/shard_map/normal_equations/pallas_call | solution.py:406
  24.0 1.5 %collective-permute-start.7 = (f32[16,128]{1,0:T(8,128)S(1)}, f32[16,128]{1,0:T(8,128)S(1)}, u32[]{:S(2)}, u32[]{:S(2)}) collective-permute-start(f32[16,128]{1,0:T(8,128)S(1)} %get-tuple-element.18.refs_0_), channel_id=1, source_target_pairs={{0,2},{2,0},{1,3},{3,1},{4,6},{6,4},{5,7},{7,5},{8,10},{10,8},{9,1... | collective-permute-start | bytes 24584 | tf_op jit(solution)/shard_map/ppermute | solution.py:533
  25.5 2.2 %collective-permute-done.7.refs_1_ = f32[16,128]{1,0:T(8,128)S(1)} collective-permute-done((f32[16,128]{1,0:T(8,128)S(1)}, f32[16,128]{1,0:T(8,128)S(1)}, u32[]{:S(2)}, u32[]{:S(2)}) %collective-permute-start.7) | collective-permute-done | bytes 8224 | tf_op jit(solution)/shard_map/ppermute | solution.py:533
  27.7 2.7 %fit.1 = bf16[16,64,256]{2,1,0:T(8,128)(2,1)} custom-call(s32[16]{0:T(128)S(1)} %get-tuple-element.17.order_ref, f32[16,128]{1,0:T(8,128)S(1)} %get-tuple-element.18.refs_0_, f32[16,128]{1,0:T(8,128)S(1)} %collective-permute-done.7.refs_1_, bf16[2,96,1024]{2,1,0:T(8,128)(2,1)S(1)} %get-tuple-element.19.refs_2_, bf16[16,64,256]{2,1,0:T(8,128)(2,1)S(1)} %bitcast.11), custom_call_target="tpu_custom_call" | custom-call | bytes 2097152 | tf_op jit(solution)/shard_map/fit/pallas_call | solution.py:406
  (14 shorter events, 0.0 us)
Async XLA Ops:
  0.6 6.1 %copy-start = (s32[1,16,64,256]{3,2,1,0:T(8,128)S(1)}, s32[1,16,64,256]{3,2,1,0:T(8,128)}, u32[]{:S(2)}) copy-start(s32[1,16,64,256]{3,2,1,0:T(8,128)} %param.8) | copy-start | bytes 3145732
  0.6 6.1 %copy-start.1 = (bf16[1,16,64,256]{3,2,1,0:T(8,128)(2,1)S(1)}, bf16[1,16,64,256]{3,2,1,0:T(8,128)(2,1)}, u32[]{:S(2)}) copy-start(bf16[1,16,64,256]{3,2,1,0:T(8,128)(2,1)} %param.7) | copy-start | bytes 1572868
  0.7 6.1 %copy-start.5 = (s32[16,1]{0,1:T(1,128)S(1)}, s32[16,1]{0,1:T(1,128)}, u32[]{:S(2)}) copy-start(s32[16,1]{0,1:T(1,128)} %param.10) | copy-start | bytes 196
  0.7 6.1 %copy-start.6 = (bf16[1,16]{1,0:T(2,128)(2,1)S(1)}, bf16[1,16]{1,0:T(2,128)(2,1)}, u32[]{:S(2)}) copy-start(bf16[1,16]{1,0:T(2,128)(2,1)} %weight_ref.1) | copy-start | bytes 100
  2.7 13.8 %copy-start.2 = (bf16[144,256]{1,0:T(8,128)(2,1)S(1)}, bf16[144,256]{1,0:T(8,128)(2,1)}, u32[]{:S(2)}) copy-start(bf16[144,256]{1,0:T(8,128)(2,1)} %first_sums.1.refs_0_) | copy-start | bytes 221188
  2.7 13.8 %copy-start.7 = (s32[4]{0:T(128)S(1)}, s32[4]{0:T(128)}, u32[]{:S(2)}) copy-start(s32[4]{0:T(128)} %owner_ref.3) | copy-start | bytes 52
  2.7 8.9 %collective-permute-start.2 = (bf16[144,256]{1,0:T(8,128)(2,1)}, bf16[144,256]{1,0:T(8,128)(2,1)S(1)}, u32[]{:S(2)}, u32[]{:S(2)}) collective-permute-start(bf16[144,256]{1,0:T(8,128)(2,1)} %first_sums.1.refs_0_), channel_id=1, source_target_pairs={{0,12},{4,0},{8,4},{12,8},{1,13},{5,1},{9,5},{13,9},{2,14},{6,2},{... | collective-permute-start | bytes 221192 | tf_op jit(solution)/shard_map/ppermute | solution.py:460
  3.2 8.4 %collective-permute-start.1 = (bf16[144,256]{1,0:T(8,128)(2,1)}, bf16[144,256]{1,0:T(8,128)(2,1)S(1)}, u32[]{:S(2)}, u32[]{:S(2)}) collective-permute-start(bf16[144,256]{1,0:T(8,128)(2,1)} %first_sums.1.refs_0_), channel_id=1, source_target_pairs={{0,8},{4,12},{8,0},{12,4},{1,9},{5,13},{9,1},{13,5},{2,10},{6,14},... | collective-permute-start | bytes 221192 | tf_op jit(solution)/shard_map/ppermute | solution.py:460
  6.7 9.8 %collective-permute-start = (bf16[144,256]{1,0:T(8,128)(2,1)}, bf16[144,256]{1,0:T(8,128)(2,1)S(1)}, u32[]{:S(2)}, u32[]{:S(2)}) collective-permute-start(bf16[144,256]{1,0:T(8,128)(2,1)} %first_sums.1.refs_0_), channel_id=1, source_target_pairs={{0,4},{4,8},{8,12},{12,0},{1,5},{5,9},{9,13},{13,1},{2,6},{6,10},{... | collective-permute-start | bytes 221192 | tf_op jit(solution)/shard_map/ppermute | solution.py:460
  7.7 12.5 %collective-permute-start.5 = (bf16[128,256]{1,0:T(8,128)(2,1)S(1)}, bf16[128,256]{1,0:T(8,128)(2,1)S(1)}, u32[]{:S(2)}, u32[]{:S(2)}) collective-permute-start(bf16[128,256]{1,0:T(8,128)(2,1)S(1)} %second_sums.1.refs_4_), channel_id=1, source_target_pairs={{0,12},{4,0},{8,4},{12,8},{1,13},{5,1},{9,5},{13,9},{2,14},{6,2},{... | collective-permute-start | bytes 196616 | tf_op jit(solution)/shard_map/ppermute | solution.py:460
  9.8 10.4 %collective-permute-start.4 = (bf16[128,256]{1,0:T(8,128)(2,1)S(1)}, bf16[128,256]{1,0:T(8,128)(2,1)S(1)}, u32[]{:S(2)}, u32[]{:S(2)}) collective-permute-start(bf16[128,256]{1,0:T(8,128)(2,1)S(1)} %second_sums.1.refs_4_), channel_id=1, source_target_pairs={{0,8},{4,12},{8,0},{12,4},{1,9},{5,13},{9,1},{13,5},{2,10},{6,14},... | collective-permute-start | bytes 196616 | tf_op jit(solution)/shard_map/ppermute | solution.py:460
  11.6 8.6 %collective-permute-start.3 = (bf16[128,256]{1,0:T(8,128)(2,1)S(1)}, bf16[128,256]{1,0:T(8,128)(2,1)S(1)}, u32[]{:S(2)}, u32[]{:S(2)}) collective-permute-start(bf16[128,256]{1,0:T(8,128)(2,1)S(1)} %second_sums.1.refs_4_), channel_id=1, source_target_pairs={{0,4},{4,8},{8,12},{12,0},{1,5},{5,9},{9,13},{13,1},{2,6},{6,10},{... | collective-permute-start | bytes 196616 | tf_op jit(solution)/shard_map/ppermute | solution.py:460
  17.2 3.8 %copy-start.3 = (bf16[3,256,256]{2,1,0:T(8,128)(2,1)S(1)}, bf16[3,256,256]{2,1,0:T(8,128)(2,1)}, u32[]{:S(2)}) copy-start(bf16[3,256,256]{2,1,0:T(8,128)(2,1)} %constant.4.clone.refs_12_) | copy-start | bytes 1179652
  17.2 3.8 %copy-start.4 = (bf16[2,192,80]{2,1,0:T(8,128)(2,1)S(1)}, bf16[2,192,80]{2,1,0:T(8,128)(2,1)}, u32[]{:S(2)}) copy-start(bf16[2,192,80]{2,1,0:T(8,128)(2,1)} %constant.5.clone.refs_11_) | copy-start | bytes 184324
  17.2 3.8 %collective-permute-start.6 = (bf16[2,16,256]{2,1,0:T(8,128)(2,1)S(1)}, bf16[2,16,256]{2,1,0:T(8,128)(2,1)S(1)}, u32[]{:S(2)}, u32[]{:S(2)}) collective-permute-start(bf16[2,16,256]{2,1,0:T(8,128)(2,1)S(1)} %get-tuple-element.12), channel_id=1, source_target_pairs={{0,2},{2,0},{1,3},{3,1},{4,6},{6,4},{5,7},{7,5},{8,10},{10,8},{9,1... | collective-permute-start | bytes 49160 | tf_op jit(solution)/shard_map/ppermute | solution.py:504
  24.0 3.7 %collective-permute-start.7 = (f32[16,128]{1,0:T(8,128)S(1)}, f32[16,128]{1,0:T(8,128)S(1)}, u32[]{:S(2)}, u32[]{:S(2)}) collective-permute-start(f32[16,128]{1,0:T(8,128)S(1)} %get-tuple-element.18.refs_0_), channel_id=1, source_target_pairs={{0,2},{2,0},{1,3},{3,1},{4,6},{6,4},{5,7},{7,5},{8,10},{10,8},{9,1... | collective-permute-start | bytes 24584 | tf_op jit(solution)/shard_map/ppermute | solution.py:533

commit v2 on v1

--- a/solution.py
+++ b/solution.py
@@ -12,6 +12,7 @@
 BASES = 6
 HALF = 9
 TILE = 16
+LANES = 128
 basis_rows = (0, 0, 1, 0, 2, 1)
 basis_cols = (0, 1, 0, 2, 0, 1)
 VMEM_LIMIT = 48 * 1024 * 1024
@@ -20,6 +21,7 @@
 VMEM = pl.BlockSpec(memory_space=pltpu.VMEM)
 SMEM = pl.BlockSpec(memory_space=pltpu.SMEM)
 HBM = pl.BlockSpec(memory_space=pltpu.HBM)
+ANY = pl.BlockSpec(memory_space=pl.ANY)
 
 
 def tap_rows():
@@ -78,7 +80,8 @@
 
 
 def put_sums(slots, cap, order_ref, weight_ref, image_of, mask_of, message_ref, base):
-    cols = message_ref.shape[1]
+    cols = image_of(0).shape[1]
+    parts = cols // LANES
     for slot in range(slots):
         numerator = jnp.zeros((TILE, cols), jnp.float32)
         denominator = jnp.zeros((TILE, cols), jnp.float32)
@@ -87,15 +90,16 @@
             weight = jnp.where(unusable(mask_of(j)), 0.0, weight_ref[j])
             denominator = denominator + weight
             numerator = numerator + weight * image_of(j).astype(jnp.float32)
-        at = base + slot * 2 * TILE
-        message_ref[at : at + TILE, :] = numerator.astype(jnp.bfloat16)
-        message_ref[at + TILE : at + 2 * TILE, :] = denominator.astype(jnp.bfloat16)
+        for kind, value in enumerate((numerator.astype(jnp.bfloat16), denominator.astype(jnp.bfloat16))):
+            for part in range(parts):
+                at = base + ((slot * 2 + kind) * parts + part) * TILE
+                message_ref[at : at + TILE, :] = value[:, part * LANES : (part + 1) * LANES]
 
 
 def first_kernel(slots, cap, half, halves, ids_hbm, weight_hbm, image_hbm, mask_hbm, message_hbm, *refs):
     message_ref, order_ref, splat_ref, ids_ref, weight_ref, image_ref, mask_ref, small_sem, sem, out_sem = refs
-    cols = image_ref.shape[2]
     tiles = half // TILE
+    step = slots * 2 * TILE * (image_ref.shape[2] // LANES)
     first = windows(half, halves)[0]
     small = [
         pltpu.make_async_copy(ids_hbm, ids_ref, small_sem.at[0]),
@@ -120,9 +124,9 @@
         copy.wait()
     piece_order(ids_ref, order_ref)
     piece_weights(weight_ref, splat_ref)
-    label_rows = message_ref.shape[0] - tiles * slots * 2 * TILE
-    line = lax.broadcasted_iota(jnp.int32, (label_rows, cols), 0)
-    labels = jnp.zeros((label_rows, cols), jnp.float32)
+    label_rows = message_ref.shape[0] - tiles * step
+    line = lax.broadcasted_iota(jnp.int32, (label_rows, LANES), 0)
+    labels = jnp.zeros((label_rows, LANES), jnp.float32)
     for slot in range(slots):
         labels = jnp.where(line == slot, ids_ref[order_ref[slot * cap]].astype(jnp.float32), labels)
     message_ref[:label_rows, :] = labels.astype(jnp.bfloat16)
@@ -131,7 +135,7 @@
         for copy in large[g]:
             copy.wait()
         here = slice(g * TILE, (g + 1) * TILE)
-        base = label_rows + g * slots * 2 * TILE
+        base = label_rows + g * step
         put_sums(
             slots,
             cap,
@@ -142,16 +146,18 @@
             message_ref,
             base,
         )
-        ready = pl.ds(done, base + slots * 2 * TILE - done)
+        ready = pl.ds(done, base + step - done)
         copies.append(pltpu.make_async_copy(message_ref.at[ready, :], message_hbm.at[ready, :], out_sem.at[g]))
         copies[-1].start()
-        done = base + slots * 2 * TILE
+        done = base + step
     for copy in copies:
         copy.wait()
 
 
-def second_kernel(slots, cap, half, ids_ref, weight_ref, image_ref, mask_ref, message_ref, order_ref, splat_ref):
+def second_kernel(slots, cap, half, ids_ref, weight_ref, image_ref, mask_ref, *refs):
+    message_ref, usable_ref, masked_ref, order_ref, splat_ref = refs
     first = windows(half, True)[1]
+    step = slots * 2 * TILE * (image_ref.shape[2] // LANES)
     piece_order(ids_ref, order_ref)
     piece_weights(weight_ref, splat_ref)
     for g in range(half // TILE):
@@ -164,13 +170,18 @@
             lambda j, here=here: image_ref[j, here, :],
             lambda j, here=here: mask_ref[j, here, :],
             message_ref,
-            g * slots * 2 * TILE,
-        )
+            g * step,
+        )
+    put_sorted(slots, cap, order_ref, image_ref, mask_ref, usable_ref, masked_ref)
 
 
 def sort_kernel(slots, cap, ids_ref, image_ref, mask_ref, usable_ref, masked_ref, order_ref):
+    piece_order(ids_ref, order_ref)
+    put_sorted(slots, cap, order_ref, image_ref, mask_ref, usable_ref, masked_ref)
+
+
+def put_sorted(slots, cap, order_ref, image_ref, mask_ref, usable_ref, masked_ref):
     rows, cols = image_ref.shape[1:]
-    piece_order(ids_ref, order_ref)
     for slot in range(slots):
         for k in range(cap):
             j = order_ref[slot * cap + k]
@@ -200,46 +211,51 @@
     return (numerator / jnp.maximum(denominator, 1.0)).astype(jnp.bfloat16)
 
 
-def combine(slots, rows, base, mine, labels, sources, put):
-    cols = sources[0].shape[1]
+def combine(slots, rows, cols, base, mine, labels, sources, put):
+    parts = cols // LANES
     labels = [value.astype(jnp.float32) for value in labels]
     hits = [[picks(label, labels[0], mine, slots, slot) for slot in range(slots)] for label in labels]
     for first in range(0, rows, TILE):
-        sums = [[jnp.zeros((TILE, cols), jnp.float32) for _ in range(2)] for _ in range(slots + 1)]
-        for d, ref in enumerate(sources):
-            for slot in range(slots):
-                for kind in range(2):
-                    at = base + first * slots * 2 + (slot * 2 + kind) * TILE
-                    value = ref[at : at + TILE, :].astype(jnp.float32)
-                    for t in range(slots + 1):
-                        if d == 0 and t < slots:
-                            if t == slot:
-                                sums[t][kind] = sums[t][kind] + value
-                        else:
-                            sums[t][kind] = sums[t][kind] + hits[d][slot][t] * value
-        for t in range(slots + 1):
-            put(t, first, quotient(*sums[t]))
+        for part in range(parts):
+            sums = [[jnp.zeros((TILE, LANES), jnp.float32) for _ in range(2)] for _ in range(slots + 1)]
+            for d, ref in enumerate(sources):
+                for slot in range(slots):
+                    for kind in range(2):
+                        at = base + (first * slots * 2 + (slot * 2 + kind) * TILE) * parts + part * TILE
+                        value = ref[at : at + TILE, :].astype(jnp.float32)
+                        for t in range(slots + 1):
+                            if d == 0 and t < slots:
+                                if t == slot:
+                                    sums[t][kind] = sums[t][kind] + value
+                            else:
+                                sums[t][kind] = sums[t][kind] + hits[d][slot][t] * value
+            lanes = slice(part * LANES, (part + 1) * LANES)
+            for t in range(slots + 1):
+                put(t, first, lanes, quotient(*sums[t]))
 
 
 def border_kernel(slots, count, rows, owner_ref, *refs):
-    sources, (template_ref, coadd_ref, edge_ref) = refs[:count], refs[count:]
-    base = sources[0].shape[0] - rows * slots * 2
+    sources, (template_ref, coadd_ref, edge_ref, mine_ref) = refs[:count], refs[count:]
+    cols = coadd_ref.shape[1]
+    base = sources[0].shape[0] - rows * slots * 2 * (cols // LANES)
     labels = [ref[:base, :] for ref in sources]
 
-    def put(t, first, value):
+    def put(t, first, lanes, value):
         if t < slots:
-            template_ref[t, first : first + TILE, :] = value
+            template_ref[t, first : first + TILE, lanes] = value
         else:
-            coadd_ref[first : first + TILE, :] = value
-
-    combine(slots, rows, base, owned_patch(owner_ref), labels, sources, put)
+            coadd_ref[first : first + TILE, lanes] = value
+
+    mine_ref[...] = jnp.broadcast_to(owned_patch(owner_ref), mine_ref.shape)
+    combine(slots, rows, cols, base, mine_ref[:1, :], labels, sources, put)
     at = pl.multiple_of((1 - lax.axis_index("strip")) * (rows - TILE), TILE)
     edge_ref[...] = template_ref[:, pl.ds(at, TILE), :]
 
 
 def gathered_kernel(slots, owner_ref, stacked_ref, template_ref, coadd_ref, edge_ref, total_ref):
     rows, cols = coadd_ref.shape
-    base = stacked_ref.shape[1] - rows * slots * 2
+    parts = cols // LANES
+    base = stacked_ref.shape[1] - rows * slots * 2 * parts
     mine = owned_patch(owner_ref)
     own_labels = stacked_ref[lax.axis_index("visit"), :base, :].astype(jnp.float32)
     total_ref[...] = jnp.zeros_like(total_ref)
@@ -250,10 +266,12 @@
             pick = picks(labels, own_labels, mine, slots, slot)
             for kind in range(2):
                 for first in range(0, rows, TILE):
-                    at = base + first * slots * 2 + (slot * 2 + kind) * TILE
-                    value = stacked_ref[d, at : at + TILE, :].astype(jnp.float32)
-                    for t in range(slots + 1):
-                        total_ref[t, kind, first : first + TILE, :] += pick[t] * value
+                    for part in range(parts):
+                        at = base + (first * slots * 2 + (slot * 2 + kind) * TILE) * parts + part * TILE
+                        value = stacked_ref[d, at : at + TILE, :].astype(jnp.float32)
+                        lanes = slice(part * LANES, (part + 1) * LANES)
+                        for t in range(slots + 1):
+                            total_ref[t, kind, first : first + TILE, lanes] += pick[t] * value
         return carry
 
     lax.fori_loop(0, stacked_ref.shape[0], add_source, 0)
@@ -264,21 +282,22 @@
     edge_ref[:, TILE:, :] = template_ref[:, rows - TILE :, :]
 
 
-def halves_kernel(slots, cap, count, rows, owner_ref, *refs):
+def halves_kernel(slots, cap, count, rows, mine_ref, *refs):
     firsts, seconds, refs = refs[:count], refs[count : 2 * count], refs[2 * count :]
     template_ref, halo_ref, coadd_ref, vertical_ref, across_ref, usable_ref, masked_ref = refs[:7]
     basis_ref, sums_ref, whole_ref, second_ref, smooth_ref, left_ref = refs[7:]
-    labels = [ref[: ref.shape[0] - rows * slots * 2, :] for ref in firsts]
+    cols = whole_ref.shape[1]
+    labels = [ref[: ref.shape[0] - rows * slots * 2 * (cols // LANES), :] for ref in firsts]
     early, late = windows(rows, True)
     whole_ref[pl.ds(early, rows), :] = coadd_ref[...]
 
-    def put(t, first, value):
+    def put(t, first, lanes, value):
         if t < slots:
-            second_ref[t, first : first + TILE, :] = value
+            second_ref[t, first : first + TILE, lanes] = value
         else:
-            whole_ref[pl.ds(late + first, TILE), :] = value
-
-    combine(slots, rows, 0, owned_patch(owner_ref), labels, seconds, put)
+            whole_ref[pl.ds(late + first, TILE), lanes] = value
+
+    combine(slots, rows, cols, 0, mine_ref[:1, :], labels, seconds, put)
     normal_equations(
         slots,
         cap,
@@ -346,8 +365,11 @@
         sums_ref[slot * cap : (slot + 1) * cap, :] = packed
 
 
-def fit_kernel(slots, cap, order_ref, *refs):
-    sums_refs, (basis_ref, image_ref, difference_hbm, difference_ref, sem) = refs[:-5], refs[-5:]
+def fit_kernel(slots, cap, order_any, *refs):
+    sums_refs, refs = refs[:-7], refs[-7:]
+    basis_ref, image_ref, difference_hbm, difference_ref, order_ref, order_sem, sem = refs
+    order_copy = pltpu.make_async_copy(order_any, order_ref, order_sem.at[0])
+    order_copy.start()
     rows, cols = image_ref.shape[1:]
     tiles = rows // TILE
     total = sums_refs[0][...]
@@ -366,9 +388,9 @@
     for k in range(BASES):
         at = k * TILE
         pivot = table[k]
-        inverse = 1.0 / pivot[:, at : at + 1]
+        inverse = 1.0 / jnp.broadcast_to(pivot[:, at : at + 1], pivot.shape)
         for c in range(k + 1, BASES + 1):
-            ratio = table[c][:, at : at + 1] * inverse
+            ratio = jnp.broadcast_to(table[c][:, at : at + 1], pivot.shape) * inverse
             table[c] = jnp.where(lanes == at, ratio, table[c] - pivot * ratio)
     spread = table[BASES]
     for step in (1, 2, 4, 8):
@@ -376,6 +398,7 @@
     line = lax.broadcasted_iota(jnp.int32, (TILE, 128), 0)
     lane = lax.broadcasted_iota(jnp.int32, (TILE, 128), 1)
     same = (line == lane % TILE) & (lane < BASES * TILE)
+    order_copy.wait()
     copies = []
     for slot in range(slots):
         blocks = [
@@ -426,11 +449,12 @@
     bf16, f32 = jnp.bfloat16, jnp.float32
     image = images[0]
     mask = mask_bits[0]
-    halves = strips == 2 and visits <= 4
+    halves = strips == 2 and visits == 4
     half = rows // 2 if halves else rows
     ids = intersection[:, 0]
     label_rows = -(-slots // TILE) * TILE
-    message_shape = (label_rows + slots * 2 * half, cols)
+    message_rows = slots * 2 * half * (cols // LANES)
+    message_shape = (label_rows + message_rows, LANES)
 
     message = call(
         functools.partial(first_kernel, slots, cap, half, halves),
@@ -455,36 +479,40 @@
         limit=FETCH_LIMIT,
     )
 
-    def everyone(value):
-        others = [
-            lax.ppermute(value, "visit", [(i, (i + shift) % visits) for i in range(visits)])
-            for shift in range(1, visits)
-        ]
-        return [value] + others
-
     sorted_shape = shape((slots, cap * TILE, tiles * cols), bf16)
+    sorted_outs = (sorted_shape, sorted_shape, shape((pieces,), jnp.int32))
     if halves:
+
+        shifts = sorted(range(1, visits), key=lambda shift: min(shift, visits - shift))
+
+        def everyone(value):
+            others = [
+                lax.ppermute(value, "visit", [(i, i ^ shift) for i in range(visits)]) for shift in shifts
+            ]
+            return [value] + others
+
         firsts = everyone(message)
-        second = call(
+        second, usable, masked, order = call(
             functools.partial(second_kernel, slots, cap, half),
             "second_sums",
-            shape((slots * 2 * half, cols), bf16),
+            (shape((message_rows, LANES), bf16), *sorted_outs),
             [SMEM] + [VMEM] * 3,
-            VMEM,
+            (VMEM,) * 3 + (SMEM,),
             (ids, visit_weight, image, mask),
-            scratch=[pltpu.SMEM((pieces,), jnp.int32), pltpu.SMEM((pieces,), f32)],
-            size=1 << 20,
+            scratch=[pltpu.SMEM((pieces,), f32)],
+            size=3 << 20,
         )
         seconds = everyone(second)
-    usable, masked, order = call(
-        functools.partial(sort_kernel, slots, cap),
-        "sorted_usable",
-        (sorted_shape, sorted_shape, shape((pieces,), jnp.int32)),
-        [SMEM, VMEM, VMEM],
-        (VMEM, VMEM, SMEM),
-        (ids, image, mask),
-        size=3 << 20,
-    )
+    else:
+        usable, masked, order = call(
+            functools.partial(sort_kernel, slots, cap),
+            "sorted_usable",
+            sorted_outs,
+            [SMEM, VMEM, VMEM],
+            (VMEM, VMEM, SMEM),
+            (ids, image, mask),
+            size=3 << 20,
+        )
     normal_outs = (shape((slots, BASES * TILE, tiles * cols), bf16), shape((pieces, 128), f32))
     normal_scratch = [
         pltpu.VMEM((3, slots, rows, cols), bf16),
@@ -492,12 +520,17 @@
     ]
     across = jnp.asarray(across_matrices(cols))
     if halves:
-        template, coadd, edge = call(
+        template, coadd, edge, mine = call(
             functools.partial(border_kernel, slots, visits, half),
             "border",
-            (shape((slots, half, cols), bf16), shape((half, cols), bf16), shape((slots, TILE, cols), bf16)),
+            (
+                shape((slots, half, cols), bf16),
+                shape((half, cols), bf16),
+                shape((slots, TILE, cols), bf16),
+                shape((8, LANES), f32),
+            ),
             [SMEM] + [VMEM] * visits,
-            (VMEM,) * 3,
+            (VMEM,) * 4,
             (patch_owner, *firsts),
             size=1 << 20,
         )
@@ -513,10 +546,10 @@
             functools.partial(halves_kernel, slots, cap, visits, half),
             "normal_equations",
             (*normal_outs, shape((rows, cols), bf16)),
-            [SMEM] + [VMEM] * (2 * visits + 7),
+            [VMEM] * (2 * visits + 8),
             (VMEM,) * 3,
             (
-                patch_owner,
+                mine,
                 *firsts,
                 *seconds,
                 template,
@@ -560,10 +593,15 @@
         functools.partial(fit_kernel, slots, cap),
         "fit",
         shape((pieces, rows, cols), bf16),
-        [SMEM] + [VMEM] * (len(totals) + 2),
+        [ANY] + [VMEM] * (len(totals) + 2),
         HBM,
         (order, *totals, basis, image),
-        scratch=[pltpu.VMEM((pieces, rows, cols), bf16), pltpu.SemaphoreType.DMA((pieces,))],
+        scratch=[
+            pltpu.VMEM((pieces, rows, cols), bf16),
+            pltpu.SMEM((pieces,), jnp.int32),
+            pltpu.SemaphoreType.DMA((1,)),
+            pltpu.SemaphoreType.DMA((pieces,)),
+        ],
         size=2 << 20,
     )
     return (coadd[None, None], difference[None])

time: 30.5 us -> 28.3 us (0.928)
  Pallas kernels: 10.8 us -> 8.84 us
  waiting for transfers between devices: 7.78 us -> 6.58 us
  starting transfers between devices: 10.9 us -> 11.9 us
    ppermute x6, waiting for transfers between devices: 4.88 us -> 2.4 us  [everyone(): lax.ppermute(value, 'visit', [(i, i ^ shift) for i in range(visits)])]
    pallas_call x6 -> x5, Pallas kernels: 10.8 us -> 8.84 us  [call(): pl.pallas_call(kernel, out_shape=outs, in_specs=in_specs, out_specs=out_s...]
    ppermute x1, waiting for transfers between devices: 0.75 us -> 2.02 us  [body(): halo = lax.ppermute(edge, 'strip', [(0, 1), (1, 0)])]
    ppermute x6, starting transfers between devices: 7.86 us -> 8.9 us  [everyone(): lax.ppermute(value, 'visit', [(i, i ^ shift) for i in range(visits)])]
  transfers between devices with their start and end apart: 8 -> 8, of which waited for: 3 -> 4; matrix products, arithmetic and copies ran while one was open for 0% -> 0% of each run, Pallas kernels for 10% -> 8%
where the time goes in v2:
time: 28.3 us; the launch traced here: 28.1 us
  starting transfers between devices  11.9 us (42%)
  Pallas kernels  8.84 us (31%)
  waiting for transfers between devices  6.58 us (23%)
  between operations  0.74 us (3%)
    ppermute x6, starting transfers between devices, everyone(): lax.ppermute(value, 'visit', [(i, i ^ shift) for i in range(visits)])  8.9 us
    pallas_call x5, Pallas kernels, call(): pl.pallas_call(kernel, out_shape=outs, in_specs=in_specs, out_specs=out_s...  8.84 us
    ppermute x6, waiting for transfers between devices, everyone(): lax.ppermute(value, 'visit', [(i, i ^ shift) for i in range(visits)])  2.4 us
    ppermute x1, waiting for transfers between devices, body(): totals = [sums, lax.ppermute(sums, 'strip', [(0, 1), (1, 0)])]  2.16 us
    ppermute x1, waiting for transfers between devices, body(): halo = lax.ppermute(edge, 'strip', [(0, 1), (1, 0)])  2.02 us
    ppermute x1, starting transfers between devices, body(): halo = lax.ppermute(edge, 'strip', [(0, 1), (1, 0)])  1.56 us
    ppermute x1, starting transfers between devices, body(): totals = [sums, lax.ppermute(sums, 'strip', [(0, 1), (1, 0)])]  1.49 us
  transfers between devices with their start and end apart: 8, of which 4 were waited for; matrix products, arithmetic and copies ran while one was open for 0% of the time, Pallas kernels for 8%

profile of v2, /device:TPU:16, one launch (start us, length us, event | category | flops | bytes accessed | tf_op | source)
XLA Modules:
  0.0 28.1 jit_solution(14378328185546421987)
XLA Ops:
  0.7 2.0 %first_sums.1.refs_0_ = bf16[272,128]{1,0:T(8,128)(2,1)} custom-call(s32[16]{0:T(128)} %bitcast.10, bf16[1,16]{1,0:T(2,128)(2,1)} %weight_ref.1, bf16[16,64,256]{2,1,0:T(8,128)(2,1)} %bitcast.5, s32[16,64,256]{2,1,0:T(8,128)} %bitcast.8), custom_call_target="tpu_custom_call" | custom-call | bytes 2097152 | tf_op jit(solution)/shard_map/first_sums/pallas_call | solution.py:429
  2.7 0.0 copy-start.2
  2.7 0.1 collective-permute-start.2
  2.8 3.0 %collective-permute-start.1 = (bf16[272,128]{1,0:T(8,128)(2,1)}, bf16[272,128]{1,0:T(8,128)(2,1)S(1)}, u32[]{:S(2)}, u32[]{:S(2)}) collective-permute-start(bf16[272,128]{1,0:T(8,128)(2,1)} %first_sums.1.refs_0_), channel_id=1, source_target_pairs={{0,12},{4,8},{8,4},{12,0},{1,13},{5,9},{9,5},{13,1},{2,14},{6,10},... | collective-permute-start | bytes 208904 | tf_op jit(solution)/shard_map/ppermute | solution.py:490
  5.8 1.3 %collective-permute-start = (bf16[272,128]{1,0:T(8,128)(2,1)}, bf16[272,128]{1,0:T(8,128)(2,1)S(1)}, u32[]{:S(2)}, u32[]{:S(2)}) collective-permute-start(bf16[272,128]{1,0:T(8,128)(2,1)} %first_sums.1.refs_0_), channel_id=1, source_target_pairs={{0,4},{4,0},{8,12},{12,8},{1,5},{5,1},{9,13},{13,9},{2,6},{6,2},{1... | collective-permute-start | bytes 208904 | tf_op jit(solution)/shard_map/ppermute | solution.py:490
  7.2 0.0 copy-start.3
  7.2 1.6 %second_sums.1 = (bf16[256,128]{1,0:T(8,128)(2,1)S(1)}, bf16[2,128,1024]{2,1,0:T(8,128)(2,1)S(1)}, bf16[2,128,1024]{2,1,0:T(8,128)(2,1)S(1)}, s32[16]{0:T(128)S(1)}) custom-call(s32[16]{0:T(128)S(1)} %bitcast.11, bf16[1,16]{1,0:T(2,128)(2,1)S(1)} %copy-done.6, bf16[16,64,256]{2,1,0:T(8,128)(2,1)S(1)} %bitcast.6, s32[16,64,256]{2,1,0:T(8,128)S(1)} %bitcast.9), custom_call_target="tpu_custom_call" | custom-call | bytes 3145728 | tf_op jit(solution)/shard_map/second_sums/pallas_call | solution.py:429
  8.8 0.0 copy-start.7
  8.8 0.0 copy-start.4
  8.8 0.2 collective-permute-start.5
  9.0 2.0 %collective-permute-start.4 = (bf16[256,128]{1,0:T(8,128)(2,1)S(1)}, bf16[256,128]{1,0:T(8,128)(2,1)S(1)}, u32[]{:S(2)}, u32[]{:S(2)}) collective-permute-start(bf16[256,128]{1,0:T(8,128)(2,1)S(1)} %get-tuple-element.14.refs_4_), channel_id=1, source_target_pairs={{0,12},{4,8},{8,4},{12,0},{1,13},{5,9},{9,5},{13,1},{2,14},{6,10},... | collective-permute-start | bytes 196616 | tf_op jit(solution)/shard_map/ppermute | solution.py:490
  11.0 0.0 collective-permute-done.2.refs_3_
  11.0 2.2 %collective-permute-start.3 = (bf16[256,128]{1,0:T(8,128)(2,1)S(1)}, bf16[256,128]{1,0:T(8,128)(2,1)S(1)}, u32[]{:S(2)}, u32[]{:S(2)}) collective-permute-start(bf16[256,128]{1,0:T(8,128)(2,1)S(1)} %get-tuple-element.14.refs_4_), channel_id=1, source_target_pairs={{0,4},{4,0},{8,12},{12,8},{1,5},{5,1},{9,13},{13,9},{2,6},{6,2},{1... | collective-permute-start | bytes 196616 | tf_op jit(solution)/shard_map/ppermute | solution.py:490
  13.3 2.2 %collective-permute-done.1.refs_2_ = bf16[272,128]{1,0:T(8,128)(2,1)S(1)} collective-permute-done((bf16[272,128]{1,0:T(8,128)(2,1)}, bf16[272,128]{1,0:T(8,128)(2,1)S(1)}, u32[]{:S(2)}, u32[]{:S(2)}) %collective-permute-start.1) | collective-permute-done | bytes 69664 | tf_op jit(solution)/shard_map/ppermute | solution.py:490
  15.5 0.0 collective-permute-done.refs_1_
  15.5 0.7 %border.1 = (bf16[2,32,256]{2,1,0:T(8,128)(2,1)S(1)}, bf16[32,256]{1,0:T(8,128)(2,1)S(1)}, bf16[2,16,256]{2,1,0:T(8,128)(2,1)S(1)}, f32[8,128]{1,0:T(8,128)S(1)}) custom-call(s32[4]{0:T(128)S(1)} %copy-done.7, bf16[272,128]{1,0:T(8,128)(2,1)S(1)} %copy-done.2, bf16[272,128]{1,0:T(8,128)(2,1)S(1)} %collective-permute-done.refs_1_, ...), custom_call_target="tpu_custom_call" | custom-call | bytes 1048576 | tf_op jit(solution)/shard_map/border/pallas_call | solution.py:429
  16.2 1.6 %collective-permute-start.6 = (bf16[2,16,256]{2,1,0:T(8,128)(2,1)S(1)}, bf16[2,16,256]{2,1,0:T(8,128)(2,1)S(1)}, u32[]{:S(2)}, u32[]{:S(2)}) collective-permute-start(bf16[2,16,256]{2,1,0:T(8,128)(2,1)S(1)} %get-tuple-element.16), channel_id=1, source_target_pairs={{0,2},{2,0},{1,3},{3,1},{4,6},{6,4},{5,7},{7,5},{8,10},{10,8},{9,1... | collective-permute-start | bytes 49160 | tf_op jit(solution)/shard_map/ppermute | solution.py:537
  17.7 0.0 collective-permute-done.5.refs_7_
  17.7 0.2 collective-permute-done.4.refs_6_
  17.9 2.0 %collective-permute-done.6.refs_9_ = bf16[2,16,256]{2,1,0:T(8,128)(2,1)S(1)} collective-permute-done((bf16[2,16,256]{2,1,0:T(8,128)(2,1)S(1)}, bf16[2,16,256]{2,1,0:T(8,128)(2,1)S(1)}, u32[]{:S(2)}, u32[]{:S(2)}) %collective-permute-start.6) | collective-permute-done | bytes 16416 | tf_op jit(solution)/shard_map/ppermute | solution.py:537
  20.0 2.5 %normal_equations.1 = (bf16[2,96,1024]{2,1,0:T(8,128)(2,1)S(1)}, f32[16,128]{1,0:T(8,128)S(1)}, bf16[64,256]{1,0:T(8,128)(2,1)}) custom-call(f32[8,128]{1,0:T(8,128)S(1)} %get-tuple-element.13.mine_ref, bf16[272,128]{1,0:T(8,128)(2,1)S(1)} %copy-done.2, bf16[272,128]{1,0:T(8,128)(2,1)S(1)} %collective-permute-done.refs_1_, ...), custom_call_target="tpu_custom_call" | custom-call | bytes 2097152 | tf_op jit(solution)/shard_map/normal_equations/pallas_call | solution.py:429
  22.5 1.5 %collective-permute-start.7 = (f32[16,128]{1,0:T(8,128)S(1)}, f32[16,128]{1,0:T(8,128)S(1)}, u32[]{:S(2)}, u32[]{:S(2)}) collective-permute-start(f32[16,128]{1,0:T(8,128)S(1)} %get-tuple-element.22.refs_0_), channel_id=1, source_target_pairs={{0,2},{2,0},{1,3},{3,1},{4,6},{6,4},{5,7},{7,5},{8,10},{10,8},{9,1... | collective-permute-start | bytes 24584 | tf_op jit(solution)/shard_map/ppermute | solution.py:566
  23.9 2.2 %collective-permute-done.7.refs_1_ = f32[16,128]{1,0:T(8,128)S(1)} collective-permute-done((f32[16,128]{1,0:T(8,128)S(1)}, f32[16,128]{1,0:T(8,128)S(1)}, u32[]{:S(2)}, u32[]{:S(2)}) %collective-permute-start.7) | collective-permute-done | bytes 8224 | tf_op jit(solution)/shard_map/ppermute | solution.py:566
  26.1 2.0 %fit.1 = bf16[16,64,256]{2,1,0:T(8,128)(2,1)} custom-call(s32[16]{0:T(128)S(1)} %get-tuple-element.21.order_any, f32[16,128]{1,0:T(8,128)S(1)} %get-tuple-element.22.refs_0_, f32[16,128]{1,0:T(8,128)S(1)} %collective-permute-done.7.refs_1_, bf16[2,96,1024]{2,1,0:T(8,128)(2,1)S(1)} %get-tuple-element.23.refs_2_, bf16[16,64,256]{2,1,0:T(8,128)(2,1)S(1)} %bitcast.7), custom_call_target="tpu_custom_call" | custom-call | bytes 2097152 | tf_op jit(solution)/shard_map/fit/pallas_call | solution.py:429
  (13 shorter events, 0.0 us)
Async XLA Ops:
  0.6 6.5 %copy-start.1 = (s32[1,16,64,256]{3,2,1,0:T(8,128)S(1)}, s32[1,16,64,256]{3,2,1,0:T(8,128)}, u32[]{:S(2)}) copy-start(s32[1,16,64,256]{3,2,1,0:T(8,128)} %param.8) | copy-start | bytes 3145732
  0.6 6.5 %copy-start = (bf16[1,16,64,256]{3,2,1,0:T(8,128)(2,1)S(1)}, bf16[1,16,64,256]{3,2,1,0:T(8,128)(2,1)}, u32[]{:S(2)}) copy-start(bf16[1,16,64,256]{3,2,1,0:T(8,128)(2,1)} %param.7) | copy-start | bytes 1572868
  0.7 6.5 %copy-start.5 = (s32[16,1]{0,1:T(1,128)S(1)}, s32[16,1]{0,1:T(1,128)}, u32[]{:S(2)}) copy-start(s32[16,1]{0,1:T(1,128)} %param.10) | copy-start | bytes 196
  0.7 6.5 %copy-start.6 = (bf16[1,16]{1,0:T(2,128)(2,1)S(1)}, bf16[1,16]{1,0:T(2,128)(2,1)}, u32[]{:S(2)}) copy-start(bf16[1,16]{1,0:T(2,128)(2,1)} %weight_ref.1) | copy-start | bytes 100
  2.7 12.8 %copy-start.2 = (bf16[272,128]{1,0:T(8,128)(2,1)S(1)}, bf16[272,128]{1,0:T(8,128)(2,1)}, u32[]{:S(2)}) copy-start(bf16[272,128]{1,0:T(8,128)(2,1)} %first_sums.1.refs_0_) | copy-start | bytes 208900
  2.7 8.3 %collective-permute-start.2 = (bf16[272,128]{1,0:T(8,128)(2,1)}, bf16[272,128]{1,0:T(8,128)(2,1)S(1)}, u32[]{:S(2)}, u32[]{:S(2)}) collective-permute-start(bf16[272,128]{1,0:T(8,128)(2,1)} %first_sums.1.refs_0_), channel_id=1, source_target_pairs={{0,8},{4,12},{8,0},{12,4},{1,9},{5,13},{9,1},{13,5},{2,10},{6,14},... | collective-permute-start | bytes 208904 | tf_op jit(solution)/shard_map/ppermute | solution.py:490
  2.8 12.7 %collective-permute-start.1 = (bf16[272,128]{1,0:T(8,128)(2,1)}, bf16[272,128]{1,0:T(8,128)(2,1)S(1)}, u32[]{:S(2)}, u32[]{:S(2)}) collective-permute-start(bf16[272,128]{1,0:T(8,128)(2,1)} %first_sums.1.refs_0_), channel_id=1, source_target_pairs={{0,12},{4,8},{8,4},{12,0},{1,13},{5,9},{9,5},{13,1},{2,14},{6,10},... | collective-permute-start | bytes 208904 | tf_op jit(solution)/shard_map/ppermute | solution.py:490
  5.8 9.7 %collective-permute-start = (bf16[272,128]{1,0:T(8,128)(2,1)}, bf16[272,128]{1,0:T(8,128)(2,1)S(1)}, u32[]{:S(2)}, u32[]{:S(2)}) collective-permute-start(bf16[272,128]{1,0:T(8,128)(2,1)} %first_sums.1.refs_0_), channel_id=1, source_target_pairs={{0,4},{4,0},{8,12},{12,8},{1,5},{5,1},{9,13},{13,9},{2,6},{6,2},{1... | collective-permute-start | bytes 208904 | tf_op jit(solution)/shard_map/ppermute | solution.py:490
  7.2 12.8 %copy-start.3 = (bf16[3,256,256]{2,1,0:T(8,128)(2,1)S(1)}, bf16[3,256,256]{2,1,0:T(8,128)(2,1)}, u32[]{:S(2)}) copy-start(bf16[3,256,256]{2,1,0:T(8,128)(2,1)} %constant.4.clone.refs_12_) | copy-start | bytes 1179652
  8.8 6.7 %copy-start.7 = (s32[4]{0:T(128)S(1)}, s32[4]{0:T(128)}, u32[]{:S(2)}) copy-start(s32[4]{0:T(128)} %owner_ref.1) | copy-start | bytes 52
  8.8 11.1 %copy-start.4 = (bf16[2,192,80]{2,1,0:T(8,128)(2,1)S(1)}, bf16[2,192,80]{2,1,0:T(8,128)(2,1)}, u32[]{:S(2)}) copy-start(bf16[2,192,80]{2,1,0:T(8,128)(2,1)} %constant.5.clone.refs_11_) | copy-start | bytes 184324
  8.8 8.9 %collective-permute-start.5 = (bf16[256,128]{1,0:T(8,128)(2,1)S(1)}, bf16[256,128]{1,0:T(8,128)(2,1)S(1)}, u32[]{:S(2)}, u32[]{:S(2)}) collective-permute-start(bf16[256,128]{1,0:T(8,128)(2,1)S(1)} %get-tuple-element.14.refs_4_), channel_id=1, source_target_pairs={{0,8},{4,12},{8,0},{12,4},{1,9},{5,13},{9,1},{13,5},{2,10},{6,14},... | collective-permute-start | bytes 196616 | tf_op jit(solution)/shard_map/ppermute | solution.py:490
  9.0 8.9 %collective-permute-start.4 = (bf16[256,128]{1,0:T(8,128)(2,1)S(1)}, bf16[256,128]{1,0:T(8,128)(2,1)S(1)}, u32[]{:S(2)}, u32[]{:S(2)}) collective-permute-start(bf16[256,128]{1,0:T(8,128)(2,1)S(1)} %get-tuple-element.14.refs_4_), channel_id=1, source_target_pairs={{0,12},{4,8},{8,4},{12,0},{1,13},{5,9},{9,5},{13,1},{2,14},{6,10},... | collective-permute-start | bytes 196616 | tf_op jit(solution)/shard_map/ppermute | solution.py:490
  11.0 6.9 %collective-permute-start.3 = (bf16[256,128]{1,0:T(8,128)(2,1)S(1)}, bf16[256,128]{1,0:T(8,128)(2,1)S(1)}, u32[]{:S(2)}, u32[]{:S(2)}) collective-permute-start(bf16[256,128]{1,0:T(8,128)(2,1)S(1)} %get-tuple-element.14.refs_4_), channel_id=1, source_target_pairs={{0,4},{4,0},{8,12},{12,8},{1,5},{5,1},{9,13},{13,9},{2,6},{6,2},{1... | collective-permute-start | bytes 196616 | tf_op jit(solution)/shard_map/ppermute | solution.py:490
  16.2 3.8 %collective-permute-start.6 = (bf16[2,16,256]{2,1,0:T(8,128)(2,1)S(1)}, bf16[2,16,256]{2,1,0:T(8,128)(2,1)S(1)}, u32[]{:S(2)}, u32[]{:S(2)}) collective-permute-start(bf16[2,16,256]{2,1,0:T(8,128)(2,1)S(1)} %get-tuple-element.16), channel_id=1, source_target_pairs={{0,2},{2,0},{1,3},{3,1},{4,6},{6,4},{5,7},{7,5},{8,10},{10,8},{9,1... | collective-permute-start | bytes 49160 | tf_op jit(solution)/shard_map/ppermute | solution.py:537
  22.5 3.7 %collective-permute-start.7 = (f32[16,128]{1,0:T(8,128)S(1)}, f32[16,128]{1,0:T(8,128)S(1)}, u32[]{:S(2)}, u32[]{:S(2)}) collective-permute-start(f32[16,128]{1,0:T(8,128)S(1)} %get-tuple-element.22.refs_0_), channel_id=1, source_target_pairs={{0,2},{2,0},{1,3},{3,1},{4,6},{6,4},{5,7},{7,5},{8,10},{10,8},{9,1... | collective-permute-start | bytes 24584 | tf_op jit(solution)/shard_map/ppermute | solution.py:566

commit v3 on v2

--- a/solution.py
+++ b/solution.py
@@ -203,7 +203,9 @@
 
 def picks(labels, own_labels, mine, slots, slot):
     label = labels[slot : slot + 1, :]
-    hits = [label == own_labels[t : t + 1, :] for t in range(slots)] + [label == mine]
+    hits = [label == own_labels[t : t + 1, :] for t in range(slots)]
+    if mine is not None:
+        hits.append(label == mine)
     return [hit.astype(jnp.float32) for hit in hits]
 
 
@@ -215,6 +217,7 @@
     parts = cols // LANES
     labels = [value.astype(jnp.float32) for value in labels]
     hits = [[picks(label, labels[0], mine, slots, slot) for slot in range(slots)] for label in labels]
+    targets = range(slots) if mine is None else range(slots, slots + 1)
     for first in range(0, rows, TILE):
         for part in range(parts):
             sums = [[jnp.zeros((TILE, LANES), jnp.float32) for _ in range(2)] for _ in range(slots + 1)]
@@ -223,33 +226,47 @@
                     for kind in range(2):
                         at = base + (first * slots * 2 + (slot * 2 + kind) * TILE) * parts + part * TILE
                         value = ref[at : at + TILE, :].astype(jnp.float32)
-                        for t in range(slots + 1):
+                        for t in targets:
                             if d == 0 and t < slots:
                                 if t == slot:
                                     sums[t][kind] = sums[t][kind] + value
                             else:
                                 sums[t][kind] = sums[t][kind] + hits[d][slot][t] * value
             lanes = slice(part * LANES, (part + 1) * LANES)
-            for t in range(slots + 1):
+            for t in targets:
                 put(t, first, lanes, quotient(*sums[t]))
 
 
-def border_kernel(slots, count, rows, owner_ref, *refs):
-    sources, (template_ref, coadd_ref, edge_ref, mine_ref) = refs[:count], refs[count:]
-    cols = coadd_ref.shape[1]
-    base = sources[0].shape[0] - rows * slots * 2 * (cols // LANES)
-    labels = [ref[:base, :] for ref in sources]
+def message_base(ref, slots, rows, cols):
+    return ref.shape[0] - slots * 2 * rows * (cols // LANES)
+
+
+def border_kernel(slots, rows, *refs):
+    sources, (template_ref, edge_ref) = refs[:-2], refs[-2:]
+    cols = template_ref.shape[2]
+    base = message_base(sources[0], slots, rows, cols)
 
     def put(t, first, lanes, value):
-        if t < slots:
-            template_ref[t, first : first + TILE, lanes] = value
-        else:
-            coadd_ref[first : first + TILE, lanes] = value
-
-    mine_ref[...] = jnp.broadcast_to(owned_patch(owner_ref), mine_ref.shape)
-    combine(slots, rows, cols, base, mine_ref[:1, :], labels, sources, put)
+        template_ref[t, first : first + TILE, lanes] = value
+
+    combine(slots, rows, cols, base, None, [ref[:base, :] for ref in sources], sources, put)
     at = pl.multiple_of((1 - lax.axis_index("strip")) * (rows - TILE), TILE)
     edge_ref[...] = template_ref[:, pl.ds(at, TILE), :]
+
+
+def own_kernel(slots, count, rows, owner_ref, after_ref, *refs):
+    firsts, seconds, coadd_ref = refs[:count], refs[count : 2 * count], refs[2 * count]
+    del after_ref
+    cols = coadd_ref.shape[1]
+    base = message_base(firsts[0], slots, rows, cols)
+    labels = [ref[:base, :] for ref in firsts]
+    mine = owned_patch(owner_ref)
+    for sources, skip, start in zip((firsts, seconds), (base, 0), windows(rows, True)):
+
+        def put(t, first, lanes, value, start=start):
+            coadd_ref[pl.ds(start + first, TILE), lanes] = value
+
+        combine(slots, rows, cols, skip, mine, labels, sources, put)
 
 
 def gathered_kernel(slots, owner_ref, stacked_ref, template_ref, coadd_ref, edge_ref, total_ref):
@@ -282,22 +299,17 @@
     edge_ref[:, TILE:, :] = template_ref[:, rows - TILE :, :]
 
 
-def halves_kernel(slots, cap, count, rows, mine_ref, *refs):
+def halves_kernel(slots, cap, count, rows, *refs):
     firsts, seconds, refs = refs[:count], refs[count : 2 * count], refs[2 * count :]
-    template_ref, halo_ref, coadd_ref, vertical_ref, across_ref, usable_ref, masked_ref = refs[:7]
-    basis_ref, sums_ref, whole_ref, second_ref, smooth_ref, left_ref = refs[7:]
-    cols = whole_ref.shape[1]
-    labels = [ref[: ref.shape[0] - rows * slots * 2 * (cols // LANES), :] for ref in firsts]
-    early, late = windows(rows, True)
-    whole_ref[pl.ds(early, rows), :] = coadd_ref[...]
+    template_ref, halo_ref, vertical_ref, across_ref, usable_ref, masked_ref = refs[:6]
+    basis_ref, sums_ref, second_ref, smooth_ref, left_ref = refs[6:]
+    cols = template_ref.shape[2]
+    base = message_base(firsts[0], slots, rows, cols)
 
     def put(t, first, lanes, value):
-        if t < slots:
-            second_ref[t, first : first + TILE, lanes] = value
-        else:
-            whole_ref[pl.ds(late + first, TILE), lanes] = value
-
-    combine(slots, rows, cols, 0, mine_ref[:1, :], labels, seconds, put)
+        second_ref[t, first : first + TILE, lanes] = value
+
+    combine(slots, rows, cols, 0, None, [ref[:base, :] for ref in firsts], seconds, put)
     normal_equations(
         slots,
         cap,
@@ -385,31 +397,47 @@
         if c < BASES:
             line = line + jnp.where(lanes == c * TILE, 1.0, 0.0)
         table.append(line)
-    for k in range(BASES):
-        at = k * TILE
-        pivot = table[k]
-        inverse = 1.0 / jnp.broadcast_to(pivot[:, at : at + 1], pivot.shape)
-        for c in range(k + 1, BASES + 1):
-            ratio = jnp.broadcast_to(table[c][:, at : at + 1], pivot.shape) * inverse
-            table[c] = jnp.where(lanes == at, ratio, table[c] - pivot * ratio)
-    spread = table[BASES]
-    for step in (1, 2, 4, 8):
-        spread = spread + pltpu.roll(spread, step, 1)
-    line = lax.broadcasted_iota(jnp.int32, (TILE, 128), 0)
-    lane = lax.broadcasted_iota(jnp.int32, (TILE, 128), 1)
-    same = (line == lane % TILE) & (lane < BASES * TILE)
+    def entry(line, a):
+        return jnp.broadcast_to(line[:, a * TILE : a * TILE + 1], line.shape)
+
+    for k in range(0, BASES, 2):
+        first, second = table[k], table[k + 1]
+        p, q, r, s = entry(first, k), entry(second, k), entry(first, k + 1), entry(second, k + 1)
+        inverse = 1.0 / (p * s - q * r)
+        for c in range(k + 2, BASES + 1):
+            above, below = entry(table[c], k), entry(table[c], k + 1)
+            x = (s * above - q * below) * inverse
+            y = (p * below - r * above) * inverse
+            rest = table[c] - (first * x + second * y)
+            table[c] = jnp.where(lanes == k * TILE, x, jnp.where(lanes == (k + 1) * TILE, y, rest))
+    exact = [entry(table[BASES], a) for a in range(BASES)]
+    high = [value.astype(jnp.bfloat16).astype(jnp.float32) for value in exact]
+    terms = high + [value - upper for value, upper in zip(exact, high)]
+    group = lanes // TILE
+    spread = []
+    for first in range(0, len(terms), LANES // TILE):
+        several = terms[first : first + LANES // TILE]
+        line = several[0]
+        for g in range(1, len(several)):
+            line = jnp.where(group >= g, several[g], line)
+        spread.append(line)
+    width = len(terms) * TILE
+    spread = jnp.concatenate(spread, axis=1)[:, :width]
+    line = lax.broadcasted_iota(jnp.int32, (TILE, width), 0)
+    lane = lax.broadcasted_iota(jnp.int32, (TILE, width), 1)
+    same = line == lane % TILE
     order_copy.wait()
     copies = []
     for slot in range(slots):
         blocks = [
-            jnp.where(same, spread[slot * cap + k : slot * cap + k + 1, :], 0.0) for k in range(cap)
+            jnp.where(same, spread[slot * cap + k : slot * cap + k + 1, :], 0.0).astype(jnp.bfloat16)
+            for k in range(cap)
         ]
-        exact = jnp.concatenate(blocks, axis=0)[:, : BASES * TILE]
-        high = exact.astype(jnp.bfloat16)
-        low = (exact - high.astype(jnp.float32)).astype(jnp.bfloat16)
         basis = basis_ref[slot]
-        fitted = jnp.dot(high, basis, preferred_element_type=jnp.float32) + jnp.dot(
-            low, basis, preferred_element_type=jnp.float32
+        fitted = jnp.dot(
+            jnp.concatenate(blocks, axis=0),
+            jnp.concatenate([basis, basis], axis=0),
+            preferred_element_type=jnp.float32,
         )
         for k in range(cap):
             j = order_ref[slot * cap + k]
@@ -520,18 +548,13 @@
     ]
     across = jnp.asarray(across_matrices(cols))
     if halves:
-        template, coadd, edge, mine = call(
-            functools.partial(border_kernel, slots, visits, half),
+        template, edge = call(
+            functools.partial(border_kernel, slots, half),
             "border",
-            (
-                shape((slots, half, cols), bf16),
-                shape((half, cols), bf16),
-                shape((slots, TILE, cols), bf16),
-                shape((8, LANES), f32),
-            ),
-            [SMEM] + [VMEM] * visits,
-            (VMEM,) * 4,
-            (patch_owner, *firsts),
+            (shape((slots, half, cols), bf16), shape((slots, TILE, cols), bf16)),
+            [VMEM] * visits,
+            (VMEM,) * 2,
+            firsts,
             size=1 << 20,
         )
         halo = lax.ppermute(edge, "strip", [(0, 1), (1, 0)])
@@ -542,26 +565,24 @@
                 vertical_matrix(rows, low + high + list(range(-TILE, 0))),
             ]
         )
-        basis, sums, coadd = call(
+        basis, sums = call(
             functools.partial(halves_kernel, slots, cap, visits, half),
             "normal_equations",
-            (*normal_outs, shape((rows, cols), bf16)),
-            [VMEM] * (2 * visits + 8),
-            (VMEM,) * 3,
-            (
-                mine,
-                *firsts,
-                *seconds,
-                template,
-                halo,
-                coadd,
-                jnp.asarray(vertical),
-                across,
-                usable,
-                masked,
-            ),
+            normal_outs,
+            [VMEM] * (2 * visits + 6),
+            (VMEM,) * 2,
+            (*firsts, *seconds, template, halo, jnp.asarray(vertical), across, usable, masked),
             scratch=[pltpu.VMEM((slots, half, cols), bf16)] + normal_scratch,
             size=2 << 20,
+        )
+        coadd = call(
+            functools.partial(own_kernel, slots, visits, half),
+            "own_patch",
+            shape((rows, cols), bf16),
+            [SMEM, ANY] + [VMEM] * (2 * visits),
+            VMEM,
+            (patch_owner, sums, *firsts, *seconds),
+            size=1 << 20,
         )
         totals = [sums, lax.ppermute(sums, "strip", [(0, 1), (1, 0)])]
     else:

time: 28.3 us -> 26.8 us (0.947)
  waiting for transfers between devices: 6.58 us -> 5.3 us
    ppermute x1, waiting for transfers between devices: 2.16 us -> 0.87 us  [body(): totals = [sums, lax.ppermute(sums, 'strip', [(0, 1), (1, 0)])]]
    ppermute x6, waiting for transfers between devices: 2.4 us -> 3 us  [everyone(): lax.ppermute(value, 'visit', [(i, i ^ shift) for i in range(visits)])]
    ppermute x1, waiting for transfers between devices: 2.02 us -> 1.43 us  [body(): halo = lax.ppermute(edge, 'strip', [(0, 1), (1, 0)])]
    pallas_call x5 -> x6, Pallas kernels: 8.84 us -> 8.58 us  [call(): pl.pallas_call(kernel, out_shape=outs, in_specs=in_specs, out_specs=out_s...]
  transfers between devices with their start and end apart: 8 -> 8, of which waited for: 4 -> 4; matrix products, arithmetic and copies ran while one was open for 0% -> 0% of each run, Pallas kernels for 8% -> 11%
where the time goes in v3:
time: 26.8 us; the launch traced here: 26.6 us
  starting transfers between devices  12 us (45%)
  Pallas kernels  8.58 us (32%)
  waiting for transfers between devices  5.3 us (20%)
  between operations  0.73 us (3%)
    ppermute x6, starting transfers between devices, everyone(): lax.ppermute(value, 'visit', [(i, i ^ shift) for i in range(visits)])  8.9 us
    pallas_call x6, Pallas kernels, call(): pl.pallas_call(kernel, out_shape=outs, in_specs=in_specs, out_specs=out_s...  8.58 us
    ppermute x6, waiting for transfers between devices, everyone(): lax.ppermute(value, 'visit', [(i, i ^ shift) for i in range(visits)])  3 us
    ppermute x1, starting transfers between devices, body(): halo = lax.ppermute(edge, 'strip', [(0, 1), (1, 0)])  1.56 us
    ppermute x1, starting transfers between devices, body(): totals = [sums, lax.ppermute(sums, 'strip', [(0, 1), (1, 0)])]  1.52 us
    ppermute x1, waiting for transfers between devices, body(): halo = lax.ppermute(edge, 'strip', [(0, 1), (1, 0)])  1.43 us
    ppermute x1, waiting for transfers between devices, body(): totals = [sums, lax.ppermute(sums, 'strip', [(0, 1), (1, 0)])]  0.87 us
  transfers between devices with their start and end apart: 8, of which 4 were waited for; matrix products, arithmetic and copies ran while one was open for 0% of the time, Pallas kernels for 11%

profile of v3, /device:TPU:16, one launch (start us, length us, event | category | flops | bytes accessed | tf_op | source)
XLA Modules:
  0.0 26.6 jit_solution(11646392288131082818)
XLA Ops:
  0.7 2.0 %first_sums.1.refs_0_ = bf16[272,128]{1,0:T(8,128)(2,1)} custom-call(s32[16]{0:T(128)} %bitcast.10, bf16[1,16]{1,0:T(2,128)(2,1)} %weight_ref.1, bf16[16,64,256]{2,1,0:T(8,128)(2,1)} %bitcast.5, s32[16,64,256]{2,1,0:T(8,128)} %bitcast.8), custom_call_target="tpu_custom_call" | custom-call | bytes 2097152 | tf_op jit(solution)/shard_map/first_sums/pallas_call | solution.py:457
  2.7 0.0 copy-start.2
  2.7 0.1 collective-permute-start.2
  2.8 3.0 %collective-permute-start.1 = (bf16[272,128]{1,0:T(8,128)(2,1)}, bf16[272,128]{1,0:T(8,128)(2,1)S(1)}, u32[]{:S(2)}, u32[]{:S(2)}) collective-permute-start(bf16[272,128]{1,0:T(8,128)(2,1)} %first_sums.1.refs_0_), channel_id=1, source_target_pairs={{0,12},{4,8},{8,4},{12,0},{1,13},{5,9},{9,5},{13,1},{2,14},{6,10},... | collective-permute-start | bytes 208904 | tf_op jit(solution)/shard_map/ppermute | solution.py:518
  5.8 1.3 %collective-permute-start = (bf16[272,128]{1,0:T(8,128)(2,1)}, bf16[272,128]{1,0:T(8,128)(2,1)S(1)}, u32[]{:S(2)}, u32[]{:S(2)}) collective-permute-start(bf16[272,128]{1,0:T(8,128)(2,1)} %first_sums.1.refs_0_), channel_id=1, source_target_pairs={{0,4},{4,0},{8,12},{12,8},{1,5},{5,1},{9,13},{13,9},{2,6},{6,2},{1... | collective-permute-start | bytes 208904 | tf_op jit(solution)/shard_map/ppermute | solution.py:518
  7.2 0.0 copy-start.3
  7.2 1.6 %second_sums.1 = (bf16[256,128]{1,0:T(8,128)(2,1)S(1)}, bf16[2,128,1024]{2,1,0:T(8,128)(2,1)S(1)}, bf16[2,128,1024]{2,1,0:T(8,128)(2,1)S(1)}, s32[16]{0:T(128)S(1)}) custom-call(s32[16]{0:T(128)S(1)} %bitcast.11, bf16[1,16]{1,0:T(2,128)(2,1)S(1)} %copy-done.6, bf16[16,64,256]{2,1,0:T(8,128)(2,1)S(1)} %bitcast.6, s32[16,64,256]{2,1,0:T(8,128)S(1)} %bitcast.9), custom_call_target="tpu_custom_call" | custom-call | bytes 3145728 | tf_op jit(solution)/shard_map/second_sums/pallas_call | solution.py:457
  8.8 0.0 copy-start.4
  8.8 0.2 collective-permute-start.5
  9.0 2.0 %collective-permute-start.4 = (bf16[256,128]{1,0:T(8,128)(2,1)S(1)}, bf16[256,128]{1,0:T(8,128)(2,1)S(1)}, u32[]{:S(2)}, u32[]{:S(2)}) collective-permute-start(bf16[256,128]{1,0:T(8,128)(2,1)S(1)} %get-tuple-element.10.refs_4_), channel_id=1, source_target_pairs={{0,12},{4,8},{8,4},{12,0},{1,13},{5,9},{9,5},{13,1},{2,14},{6,10},... | collective-permute-start | bytes 196616 | tf_op jit(solution)/shard_map/ppermute | solution.py:518
  11.0 0.0 collective-permute-done.2.refs_3_
  11.0 2.2 %collective-permute-start.3 = (bf16[256,128]{1,0:T(8,128)(2,1)S(1)}, bf16[256,128]{1,0:T(8,128)(2,1)S(1)}, u32[]{:S(2)}, u32[]{:S(2)}) collective-permute-start(bf16[256,128]{1,0:T(8,128)(2,1)S(1)} %get-tuple-element.10.refs_4_), channel_id=1, source_target_pairs={{0,4},{4,0},{8,12},{12,8},{1,5},{5,1},{9,13},{13,9},{2,6},{6,2},{1... | collective-permute-start | bytes 196616 | tf_op jit(solution)/shard_map/ppermute | solution.py:518
  13.3 2.2 %collective-permute-done.1.refs_2_ = bf16[272,128]{1,0:T(8,128)(2,1)S(1)} collective-permute-done((bf16[272,128]{1,0:T(8,128)(2,1)}, bf16[272,128]{1,0:T(8,128)(2,1)S(1)}, u32[]{:S(2)}, u32[]{:S(2)}) %collective-permute-start.1) | collective-permute-done | bytes 69664 | tf_op jit(solution)/shard_map/ppermute | solution.py:518
  15.5 0.0 collective-permute-done.refs_1_
  15.5 0.1 border.1
  15.6 1.6 %collective-permute-start.6 = (bf16[2,16,256]{2,1,0:T(8,128)(2,1)S(1)}, bf16[2,16,256]{2,1,0:T(8,128)(2,1)S(1)}, u32[]{:S(2)}, u32[]{:S(2)}) collective-permute-start(bf16[2,16,256]{2,1,0:T(8,128)(2,1)S(1)} %get-tuple-element.12), channel_id=1, source_target_pairs={{0,2},{2,0},{1,3},{3,1},{4,6},{6,4},{5,7},{7,5},{8,10},{10,8},{9,1... | collective-permute-start | bytes 49160 | tf_op jit(solution)/shard_map/ppermute | solution.py:560
  17.1 0.0 collective-permute-done.5.refs_7_
  17.1 0.8 %collective-permute-done.4.refs_6_ = bf16[256,128]{1,0:T(8,128)(2,1)S(1)} collective-permute-done((bf16[256,128]{1,0:T(8,128)(2,1)S(1)}, bf16[256,128]{1,0:T(8,128)(2,1)S(1)}, u32[]{:S(2)}, u32[]{:S(2)}) %collective-permute-start.4) | collective-permute-done | bytes 65568 | tf_op jit(solution)/shard_map/ppermute | solution.py:518
  17.9 1.4 %collective-permute-done.6.refs_9_ = bf16[2,16,256]{2,1,0:T(8,128)(2,1)S(1)} collective-permute-done((bf16[2,16,256]{2,1,0:T(8,128)(2,1)S(1)}, bf16[2,16,256]{2,1,0:T(8,128)(2,1)S(1)}, u32[]{:S(2)}, u32[]{:S(2)}) %collective-permute-start.6) | collective-permute-done | bytes 16416 | tf_op jit(solution)/shard_map/ppermute | solution.py:560
  19.4 1.9 %normal_equations.1 = (bf16[2,96,1024]{2,1,0:T(8,128)(2,1)S(1)}, f32[16,128]{1,0:T(8,128)S(1)}) custom-call(bf16[272,128]{1,0:T(8,128)(2,1)S(1)} %copy-done.2, bf16[272,128]{1,0:T(8,128)(2,1)S(1)} %collective-permute-done.refs_1_, bf16[272,128]{1,0:T(8,128)(2,1)S(1)} %collective-permute-done.1.refs_2_, bf16[272,128]{1,0:T(8,128)(2,1)S(1)} %collective-permute-done.2.refs_3_, ...), custom_call_target="tpu_custom_call" | custom-call | bytes 2097152 | tf_op jit(solution)/shard_map/normal_equations/pallas_call | solution.py:457
  21.3 1.5 %collective-permute-start.7 = (f32[16,128]{1,0:T(8,128)S(1)}, f32[16,128]{1,0:T(8,128)S(1)}, u32[]{:S(2)}, u32[]{:S(2)}) collective-permute-start(f32[16,128]{1,0:T(8,128)S(1)} %get-tuple-element.15.after_ref.refs_0_), channel_id=1, source_target_pairs={{0,2},{2,0},{1,3},{3,1},{4,6},{6,4},{5,7},{7,5},{8,10},{10,8},{9,1... | collective-permute-start | bytes 24584 | tf_op jit(solution)/shard_map/ppermute | solution.py:587
  22.8 1.3 %own_patch.1 = bf16[64,256]{1,0:T(8,128)(2,1)} custom-call(s32[4]{0:T(128)S(1)} %copy-done.7, f32[16,128]{1,0:T(8,128)S(1)} %get-tuple-element.15.after_ref.refs_0_, bf16[272,128]{1,0:T(8,128)(2,1)S(1)} %copy-done.2, bf16[272,128]{1,0:T(8,128)(2,1)S(1)} %collective-permute-done.refs_1_, bf16[272,128]{1,0:T(8,128)(2,1)S(1)} %collective-permute-done.1.refs_2_, ...), custom_call_target="tpu_custom_call" | custom-call | bytes 1048576 | tf_op jit(solution)/shard_map/own_patch/pallas_call | solution.py:457
  24.1 0.9 %collective-permute-done.7.refs_1_ = f32[16,128]{1,0:T(8,128)S(1)} collective-permute-done((f32[16,128]{1,0:T(8,128)S(1)}, f32[16,128]{1,0:T(8,128)S(1)}, u32[]{:S(2)}, u32[]{:S(2)}) %collective-permute-start.7) | collective-permute-done | bytes 8224 | tf_op jit(solution)/shard_map/ppermute | solution.py:587
  25.0 1.7 %fit.1 = bf16[16,64,256]{2,1,0:T(8,128)(2,1)} custom-call(s32[16]{0:T(128)S(1)} %get-tuple-element.16.order_any, f32[16,128]{1,0:T(8,128)S(1)} %get-tuple-element.15.after_ref.refs_0_, f32[16,128]{1,0:T(8,128)S(1)} %collective-permute-done.7.refs_1_, bf16[2,96,1024]{2,1,0:T(8,128)(2,1)S(1)} %get-tuple-element.17.refs_2_, bf16[16,64,256]{2,1,0:T(8,128)(2,1)S(1)} %bitcast.7), custom_call_target="tpu_custom_call" | custom-call | bytes 2097152 | tf_op jit(solution)/shard_map/fit/pallas_call | solution.py:457
  (14 shorter events, 0.0 us)
Async XLA Ops:
  0.6 6.5 %copy-start.1 = (s32[1,16,64,256]{3,2,1,0:T(8,128)S(1)}, s32[1,16,64,256]{3,2,1,0:T(8,128)}, u32[]{:S(2)}) copy-start(s32[1,16,64,256]{3,2,1,0:T(8,128)} %param.8) | copy-start | bytes 3145732
  0.6 6.5 %copy-start = (bf16[1,16,64,256]{3,2,1,0:T(8,128)(2,1)S(1)}, bf16[1,16,64,256]{3,2,1,0:T(8,128)(2,1)}, u32[]{:S(2)}) copy-start(bf16[1,16,64,256]{3,2,1,0:T(8,128)(2,1)} %param.7) | copy-start | bytes 1572868
  0.7 6.5 %copy-start.5 = (s32[16,1]{0,1:T(1,128)S(1)}, s32[16,1]{0,1:T(1,128)}, u32[]{:S(2)}) copy-start(s32[16,1]{0,1:T(1,128)} %param.10) | copy-start | bytes 196
  0.7 6.5 %copy-start.6 = (bf16[1,16]{1,0:T(2,128)(2,1)S(1)}, bf16[1,16]{1,0:T(2,128)(2,1)}, u32[]{:S(2)}) copy-start(bf16[1,16]{1,0:T(2,128)(2,1)} %weight_ref.1) | copy-start | bytes 100
  2.7 12.8 %copy-start.2 = (bf16[272,128]{1,0:T(8,128)(2,1)S(1)}, bf16[272,128]{1,0:T(8,128)(2,1)}, u32[]{:S(2)}) copy-start(bf16[272,128]{1,0:T(8,128)(2,1)} %first_sums.1.refs_0_) | copy-start | bytes 208900
  2.7 8.3 %collective-permute-start.2 = (bf16[272,128]{1,0:T(8,128)(2,1)}, bf16[272,128]{1,0:T(8,128)(2,1)S(1)}, u32[]{:S(2)}, u32[]{:S(2)}) collective-permute-start(bf16[272,128]{1,0:T(8,128)(2,1)} %first_sums.1.refs_0_), channel_id=1, source_target_pairs={{0,8},{4,12},{8,0},{12,4},{1,9},{5,13},{9,1},{13,5},{2,10},{6,14},... | collective-permute-start | bytes 208904 | tf_op jit(solution)/shard_map/ppermute | solution.py:518
  2.8 12.7 %collective-permute-start.1 = (bf16[272,128]{1,0:T(8,128)(2,1)}, bf16[272,128]{1,0:T(8,128)(2,1)S(1)}, u32[]{:S(2)}, u32[]{:S(2)}) collective-permute-start(bf16[272,128]{1,0:T(8,128)(2,1)} %first_sums.1.refs_0_), channel_id=1, source_target_pairs={{0,12},{4,8},{8,4},{12,0},{1,13},{5,9},{9,5},{13,1},{2,14},{6,10},... | collective-permute-start | bytes 208904 | tf_op jit(solution)/shard_map/ppermute | solution.py:518
  5.8 9.7 %collective-permute-start = (bf16[272,128]{1,0:T(8,128)(2,1)}, bf16[272,128]{1,0:T(8,128)(2,1)S(1)}, u32[]{:S(2)}, u32[]{:S(2)}) collective-permute-start(bf16[272,128]{1,0:T(8,128)(2,1)} %first_sums.1.refs_0_), channel_id=1, source_target_pairs={{0,4},{4,0},{8,12},{12,8},{1,5},{5,1},{9,13},{13,9},{2,6},{6,2},{1... | collective-permute-start | bytes 208904 | tf_op jit(solution)/shard_map/ppermute | solution.py:518
  7.2 12.2 %copy-start.3 = (bf16[3,256,256]{2,1,0:T(8,128)(2,1)S(1)}, bf16[3,256,256]{2,1,0:T(8,128)(2,1)}, u32[]{:S(2)}) copy-start(bf16[3,256,256]{2,1,0:T(8,128)(2,1)} %constant.4.clone.refs_11_) | copy-start | bytes 1179652
  8.8 10.6 %copy-start.4 = (bf16[2,192,80]{2,1,0:T(8,128)(2,1)S(1)}, bf16[2,192,80]{2,1,0:T(8,128)(2,1)}, u32[]{:S(2)}) copy-start(bf16[2,192,80]{2,1,0:T(8,128)(2,1)} %constant.5.clone.refs_10_) | copy-start | bytes 184324
  8.8 8.3 %collective-permute-start.5 = (bf16[256,128]{1,0:T(8,128)(2,1)S(1)}, bf16[256,128]{1,0:T(8,128)(2,1)S(1)}, u32[]{:S(2)}, u32[]{:S(2)}) collective-permute-start(bf16[256,128]{1,0:T(8,128)(2,1)S(1)} %get-tuple-element.10.refs_4_), channel_id=1, source_target_pairs={{0,8},{4,12},{8,0},{12,4},{1,9},{5,13},{9,1},{13,5},{2,10},{6,14},... | collective-permute-start | bytes 196616 | tf_op jit(solution)/shard_map/ppermute | solution.py:518
  9.0 8.9 %collective-permute-start.4 = (bf16[256,128]{1,0:T(8,128)(2,1)S(1)}, bf16[256,128]{1,0:T(8,128)(2,1)S(1)}, u32[]{:S(2)}, u32[]{:S(2)}) collective-permute-start(bf16[256,128]{1,0:T(8,128)(2,1)S(1)} %get-tuple-element.10.refs_4_), channel_id=1, source_target_pairs={{0,12},{4,8},{8,4},{12,0},{1,13},{5,9},{9,5},{13,1},{2,14},{6,10},... | collective-permute-start | bytes 196616 | tf_op jit(solution)/shard_map/ppermute | solution.py:518
  11.0 6.9 %collective-permute-start.3 = (bf16[256,128]{1,0:T(8,128)(2,1)S(1)}, bf16[256,128]{1,0:T(8,128)(2,1)S(1)}, u32[]{:S(2)}, u32[]{:S(2)}) collective-permute-start(bf16[256,128]{1,0:T(8,128)(2,1)S(1)} %get-tuple-element.10.refs_4_), channel_id=1, source_target_pairs={{0,4},{4,0},{8,12},{12,8},{1,5},{5,1},{9,13},{13,9},{2,6},{6,2},{1... | collective-permute-start | bytes 196616 | tf_op jit(solution)/shard_map/ppermute | solution.py:518
  15.6 3.8 %collective-permute-start.6 = (bf16[2,16,256]{2,1,0:T(8,128)(2,1)S(1)}, bf16[2,16,256]{2,1,0:T(8,128)(2,1)S(1)}, u32[]{:S(2)}, u32[]{:S(2)}) collective-permute-start(bf16[2,16,256]{2,1,0:T(8,128)(2,1)S(1)} %get-tuple-element.12), channel_id=1, source_target_pairs={{0,2},{2,0},{1,3},{3,1},{4,6},{6,4},{5,7},{7,5},{8,10},{10,8},{9,1... | collective-permute-start | bytes 49160 | tf_op jit(solution)/shard_map/ppermute | solution.py:560
  21.3 1.5 %copy-start.7 = (s32[4]{0:T(128)S(1)}, s32[4]{0:T(128)}, u32[]{:S(2)}) copy-start(s32[4]{0:T(128)} %owner_ref.1) | copy-start | bytes 52
  21.3 3.7 %collective-permute-start.7 = (f32[16,128]{1,0:T(8,128)S(1)}, f32[16,128]{1,0:T(8,128)S(1)}, u32[]{:S(2)}, u32[]{:S(2)}) collective-permute-start(f32[16,128]{1,0:T(8,128)S(1)} %get-tuple-element.15.after_ref.refs_0_), channel_id=1, source_target_pairs={{0,2},{2,0},{1,3},{3,1},{4,6},{6,4},{5,7},{7,5},{8,10},{10,8},{9,1... | collective-permute-start | bytes 24584 | tf_op jit(solution)/shard_map/ppermute | solution.py:587

commit v4 on v3

--- a/solution.py
+++ b/solution.py
@@ -155,7 +155,7 @@
 
 
 def second_kernel(slots, cap, half, ids_ref, weight_ref, image_ref, mask_ref, *refs):
-    message_ref, usable_ref, masked_ref, order_ref, splat_ref = refs
+    message_ref, order_ref, splat_ref = refs
     first = windows(half, True)[1]
     step = slots * 2 * TILE * (image_ref.shape[2] // LANES)
     piece_order(ids_ref, order_ref)
@@ -172,7 +172,6 @@
             message_ref,
             g * step,
         )
-    put_sorted(slots, cap, order_ref, image_ref, mask_ref, usable_ref, masked_ref)
 
 
 def sort_kernel(slots, cap, ids_ref, image_ref, mask_ref, usable_ref, masked_ref, order_ref):
@@ -520,27 +519,26 @@
             return [value] + others
 
         firsts = everyone(message)
-        second, usable, masked, order = call(
+        second = call(
             functools.partial(second_kernel, slots, cap, half),
             "second_sums",
-            (shape((message_rows, LANES), bf16), *sorted_outs),
+            shape((message_rows, LANES), bf16),
             [SMEM] + [VMEM] * 3,
-            (VMEM,) * 3 + (SMEM,),
+            VMEM,
             (ids, visit_weight, image, mask),
-            scratch=[pltpu.SMEM((pieces,), f32)],
-            size=3 << 20,
+            scratch=[pltpu.SMEM((pieces,), jnp.int32), pltpu.SMEM((pieces,), f32)],
+            size=1 << 20,
         )
         seconds = everyone(second)
-    else:
-        usable, masked, order = call(
-            functools.partial(sort_kernel, slots, cap),
-            "sorted_usable",
-            sorted_outs,
-            [SMEM, VMEM, VMEM],
-            (VMEM, VMEM, SMEM),
-            (ids, image, mask),
-            size=3 << 20,
-        )
+    usable, masked, order = call(
+        functools.partial(sort_kernel, slots, cap),
+        "sorted_usable",
+        sorted_outs,
+        [SMEM, VMEM, VMEM],
+        (VMEM, VMEM, SMEM),
+        (ids, image, mask),
+        size=3 << 20,
+    )
     normal_outs = (shape((slots, BASES * TILE, tiles * cols), bf16), shape((pieces, 128), f32))
     normal_scratch = [
         pltpu.VMEM((3, slots, rows, cols), bf16),

time: 26.8 us -> 26.8 us (level)
  waiting for transfers between devices: 5.3 us -> 3.06 us
  starting transfers between devices: 12 us -> 13.4 us
  Pallas kernels: 8.58 us -> 9.41 us
    ppermute x6, waiting for transfers between devices: 3 us -> 1.45 us  [everyone(): lax.ppermute(value, 'visit', [(i, i ^ shift) for i in range(visits)])]
    ppermute x6, starting transfers between devices: 8.9 us -> 10.3 us  [everyone(): lax.ppermute(value, 'visit', [(i, i ^ shift) for i in range(visits)])]
    pallas_call x6 -> x7, Pallas kernels: 8.58 us -> 9.41 us  [call(): pl.pallas_call(kernel, out_shape=outs, in_specs=in_specs, out_specs=out_s...]
    ppermute x1, waiting for transfers between devices: 1.43 us -> 0.75 us  [body(): halo = lax.ppermute(edge, 'strip', [(0, 1), (1, 0)])]
  transfers between devices with their start and end apart: 8 -> 8, of which waited for: 4 -> 3; matrix products, arithmetic and copies ran while one was open for 0% -> 0% of each run, Pallas kernels for 11% -> 14%
where the time goes in v4:
time: 26.8 us; the launch traced here: 26.7 us
  starting transfers between devices  13.4 us (50%)
  Pallas kernels  9.41 us (35%)
  waiting for transfers between devices  3.06 us (11%)
  between operations  0.75 us (3%)
    ppermute x6, starting transfers between devices, everyone(): lax.ppermute(value, 'visit', [(i, i ^ shift) for i in range(visits)])  10.3 us
    pallas_call x7, Pallas kernels, call(): pl.pallas_call(kernel, out_shape=outs, in_specs=in_specs, out_specs=out_s...  9.41 us
    ppermute x1, starting transfers between devices, body(): halo = lax.ppermute(edge, 'strip', [(0, 1), (1, 0)])  1.56 us
    ppermute x1, starting transfers between devices, body(): totals = [sums, lax.ppermute(sums, 'strip', [(0, 1), (1, 0)])]  1.51 us
    ppermute x6, waiting for transfers between devices, everyone(): lax.ppermute(value, 'visit', [(i, i ^ shift) for i in range(visits)])  1.45 us
    ppermute x1, waiting for transfers between devices, body(): totals = [sums, lax.ppermute(sums, 'strip', [(0, 1), (1, 0)])]  0.87 us
    ppermute x1, waiting for transfers between devices, body(): halo = lax.ppermute(edge, 'strip', [(0, 1), (1, 0)])  0.75 us
  transfers between devices with their start and end apart: 8, of which 3 were waited for; matrix products, arithmetic and copies ran while one was open for 0% of the time, Pallas kernels for 14%

profile of v4, /device:TPU:16, one launch (start us, length us, event | category | flops | bytes accessed | tf_op | source)
XLA Modules:
  0.0 26.7 jit_solution(1288244577090532665)
XLA Ops:
  0.7 2.0 %first_sums.1.refs_0_ = bf16[272,128]{1,0:T(8,128)(2,1)} custom-call(s32[16]{0:T(128)} %bitcast.12, bf16[1,16]{1,0:T(2,128)(2,1)} %weight_ref.1, bf16[16,64,256]{2,1,0:T(8,128)(2,1)} %bitcast.8, s32[16,64,256]{2,1,0:T(8,128)} %bitcast.5), custom_call_target="tpu_custom_call" | custom-call | bytes 2097152 | tf_op jit(solution)/shard_map/first_sums/pallas_call | solution.py:456
  2.7 0.0 copy-start.2
  2.7 0.1 collective-permute-start.2
  2.8 3.0 %collective-permute-start.1 = (bf16[272,128]{1,0:T(8,128)(2,1)}, bf16[272,128]{1,0:T(8,128)(2,1)S(1)}, u32[]{:S(2)}, u32[]{:S(2)}) collective-permute-start(bf16[272,128]{1,0:T(8,128)(2,1)} %first_sums.1.refs_0_), channel_id=1, source_target_pairs={{0,12},{4,8},{8,4},{12,0},{1,13},{5,9},{9,5},{13,1},{2,14},{6,10},... | collective-permute-start | bytes 208904 | tf_op jit(solution)/shard_map/ppermute | solution.py:517
  5.8 1.3 %collective-permute-start = (bf16[272,128]{1,0:T(8,128)(2,1)}, bf16[272,128]{1,0:T(8,128)(2,1)S(1)}, u32[]{:S(2)}, u32[]{:S(2)}) collective-permute-start(bf16[272,128]{1,0:T(8,128)(2,1)} %first_sums.1.refs_0_), channel_id=1, source_target_pairs={{0,4},{4,0},{8,12},{12,8},{1,5},{5,1},{9,13},{13,9},{2,6},{6,2},{1... | collective-permute-start | bytes 208904 | tf_op jit(solution)/shard_map/ppermute | solution.py:517
  7.2 1.0 %second_sums.1.refs_4_ = bf16[256,128]{1,0:T(8,128)(2,1)S(1)} custom-call(s32[16]{0:T(128)S(1)} %bitcast.13, bf16[1,16]{1,0:T(2,128)(2,1)S(1)} %copy-done.6, bf16[16,64,256]{2,1,0:T(8,128)(2,1)S(1)} %bitcast.9, s32[16,64,256]{2,1,0:T(8,128)S(1)} %bitcast.6), custom_call_target="tpu_custom_call" | custom-call | bytes 1048576 | tf_op jit(solution)/shard_map/second_sums/pallas_call | solution.py:456
  8.2 0.2 collective-permute-start.5
  8.3 2.0 %collective-permute-start.4 = (bf16[256,128]{1,0:T(8,128)(2,1)S(1)}, bf16[256,128]{1,0:T(8,128)(2,1)S(1)}, u32[]{:S(2)}, u32[]{:S(2)}) collective-permute-start(bf16[256,128]{1,0:T(8,128)(2,1)S(1)} %second_sums.1.refs_4_), channel_id=1, source_target_pairs={{0,12},{4,8},{8,4},{12,0},{1,13},{5,9},{9,5},{13,1},{2,14},{6,10},... | collective-permute-start | bytes 196616 | tf_op jit(solution)/shard_map/ppermute | solution.py:517
  10.4 0.0 collective-permute-done.2.refs_3_
  10.4 3.7 %collective-permute-start.3 = (bf16[256,128]{1,0:T(8,128)(2,1)S(1)}, bf16[256,128]{1,0:T(8,128)(2,1)S(1)}, u32[]{:S(2)}, u32[]{:S(2)}) collective-permute-start(bf16[256,128]{1,0:T(8,128)(2,1)S(1)} %second_sums.1.refs_4_), channel_id=1, source_target_pairs={{0,4},{4,0},{8,12},{12,8},{1,5},{5,1},{9,13},{13,9},{2,6},{6,2},{1... | collective-permute-start | bytes 196616 | tf_op jit(solution)/shard_map/ppermute | solution.py:517
  14.0 1.4 %collective-permute-done.1.refs_2_ = bf16[272,128]{1,0:T(8,128)(2,1)S(1)} collective-permute-done((bf16[272,128]{1,0:T(8,128)(2,1)}, bf16[272,128]{1,0:T(8,128)(2,1)S(1)}, u32[]{:S(2)}, u32[]{:S(2)}) %collective-permute-start.1) | collective-permute-done | bytes 69664 | tf_op jit(solution)/shard_map/ppermute | solution.py:517
  15.5 0.0 collective-permute-done.refs_1_
  15.5 0.1 border.1
  15.6 0.0 copy-start.3
  15.6 0.0 copy-start.4
  15.6 1.6 %collective-permute-start.6 = (bf16[2,16,256]{2,1,0:T(8,128)(2,1)S(1)}, bf16[2,16,256]{2,1,0:T(8,128)(2,1)S(1)}, u32[]{:S(2)}, u32[]{:S(2)}) collective-permute-start(bf16[2,16,256]{2,1,0:T(8,128)(2,1)S(1)} %get-tuple-element.10), channel_id=1, source_target_pairs={{0,2},{2,0},{1,3},{3,1},{4,6},{6,4},{5,7},{7,5},{8,10},{10,8},{9,1... | collective-permute-start | bytes 49160 | tf_op jit(solution)/shard_map/ppermute | solution.py:558
  17.2 1.5 %sorted_usable.1 = (bf16[2,128,1024]{2,1,0:T(8,128)(2,1)S(1)}, bf16[2,128,1024]{2,1,0:T(8,128)(2,1)S(1)}, s32[16]{0:T(128)S(1)}) custom-call(s32[16]{0:T(128)S(1)} %bitcast.14, bf16[16,64,256]{2,1,0:T(8,128)(2,1)S(1)} %bitcast.10, s32[16,64,256]{2,1,0:T(8,128)S(1)} %bitcast.7), custom_call_target="tpu_custom_call" | custom-call | bytes 3145728 | tf_op jit(solution)/shard_map/sorted_usable/pallas_call | solution.py:456
  18.6 0.0 collective-permute-done.5.refs_7_
  18.7 0.7 %collective-permute-done.6.refs_9_ = bf16[2,16,256]{2,1,0:T(8,128)(2,1)S(1)} collective-permute-done((bf16[2,16,256]{2,1,0:T(8,128)(2,1)S(1)}, bf16[2,16,256]{2,1,0:T(8,128)(2,1)S(1)}, u32[]{:S(2)}, u32[]{:S(2)}) %collective-permute-start.6) | collective-permute-done | bytes 16416 | tf_op jit(solution)/shard_map/ppermute | solution.py:558
  19.4 1.9 %normal_equations.1 = (bf16[2,96,1024]{2,1,0:T(8,128)(2,1)S(1)}, f32[16,128]{1,0:T(8,128)S(1)}) custom-call(bf16[272,128]{1,0:T(8,128)(2,1)S(1)} %copy-done.2, bf16[272,128]{1,0:T(8,128)(2,1)S(1)} %collective-permute-done.refs_1_, bf16[272,128]{1,0:T(8,128)(2,1)S(1)} %collective-permute-done.1.refs_2_, bf16[272,128]{1,0:T(8,128)(2,1)S(1)} %collective-permute-done.2.refs_3_, ...), custom_call_target="tpu_custom_call" | custom-call | bytes 2097152 | tf_op jit(solution)/shard_map/normal_equations/pallas_call | solution.py:456
  21.3 1.5 %collective-permute-start.7 = (f32[16,128]{1,0:T(8,128)S(1)}, f32[16,128]{1,0:T(8,128)S(1)}, u32[]{:S(2)}, u32[]{:S(2)}) collective-permute-start(f32[16,128]{1,0:T(8,128)S(1)} %get-tuple-element.13.after_ref.refs_0_), channel_id=1, source_target_pairs={{0,2},{2,0},{1,3},{3,1},{4,6},{6,4},{5,7},{7,5},{8,10},{10,8},{9,1... | collective-permute-start | bytes 24584 | tf_op jit(solution)/shard_map/ppermute | solution.py:585
  22.8 1.3 %own_patch.1 = bf16[64,256]{1,0:T(8,128)(2,1)} custom-call(s32[4]{0:T(128)S(1)} %copy-done.7, f32[16,128]{1,0:T(8,128)S(1)} %get-tuple-element.13.after_ref.refs_0_, bf16[272,128]{1,0:T(8,128)(2,1)S(1)} %copy-done.2, bf16[272,128]{1,0:T(8,128)(2,1)S(1)} %collective-permute-done.refs_1_, bf16[272,128]{1,0:T(8,128)(2,1)S(1)} %collective-permute-done.1.refs_2_, ...), custom_call_target="tpu_custom_call" | custom-call | bytes 1048576 | tf_op jit(solution)/shard_map/own_patch/pallas_call | solution.py:456
  24.1 0.9 %collective-permute-done.7.refs_1_ = f32[16,128]{1,0:T(8,128)S(1)} collective-permute-done((f32[16,128]{1,0:T(8,128)S(1)}, f32[16,128]{1,0:T(8,128)S(1)}, u32[]{:S(2)}, u32[]{:S(2)}) %collective-permute-start.7) | collective-permute-done | bytes 8224 | tf_op jit(solution)/shard_map/ppermute | solution.py:585
  25.0 1.7 %fit.1 = bf16[16,64,256]{2,1,0:T(8,128)(2,1)} custom-call(s32[16]{0:T(128)S(1)} %get-tuple-element.14.order_any, f32[16,128]{1,0:T(8,128)S(1)} %get-tuple-element.13.after_ref.refs_0_, f32[16,128]{1,0:T(8,128)S(1)} %collective-permute-done.7.refs_1_, bf16[2,96,1024]{2,1,0:T(8,128)(2,1)S(1)} %get-tuple-element.15.refs_2_, bf16[16,64,256]{2,1,0:T(8,128)(2,1)S(1)} %bitcast.11), custom_call_target="tpu_custom_call" | custom-call | bytes 2097152 | tf_op jit(solution)/shard_map/fit/pallas_call | solution.py:456
  (15 shorter events, 0.0 us)
Async XLA Ops:
  0.6 6.5 %copy-start = (s32[1,16,64,256]{3,2,1,0:T(8,128)S(1)}, s32[1,16,64,256]{3,2,1,0:T(8,128)}, u32[]{:S(2)}) copy-start(s32[1,16,64,256]{3,2,1,0:T(8,128)} %param.8) | copy-start | bytes 3145732
  0.6 6.5 %copy-start.1 = (bf16[1,16,64,256]{3,2,1,0:T(8,128)(2,1)S(1)}, bf16[1,16,64,256]{3,2,1,0:T(8,128)(2,1)}, u32[]{:S(2)}) copy-start(bf16[1,16,64,256]{3,2,1,0:T(8,128)(2,1)} %param.7) | copy-start | bytes 1572868
  0.7 6.5 %copy-start.5 = (s32[16,1]{0,1:T(1,128)S(1)}, s32[16,1]{0,1:T(1,128)}, u32[]{:S(2)}) copy-start(s32[16,1]{0,1:T(1,128)} %param.10) | copy-start | bytes 196
  0.7 6.5 %copy-start.6 = (bf16[1,16]{1,0:T(2,128)(2,1)S(1)}, bf16[1,16]{1,0:T(2,128)(2,1)}, u32[]{:S(2)}) copy-start(bf16[1,16]{1,0:T(2,128)(2,1)} %weight_ref.1) | copy-start | bytes 100
  2.7 12.8 %copy-start.2 = (bf16[272,128]{1,0:T(8,128)(2,1)S(1)}, bf16[272,128]{1,0:T(8,128)(2,1)}, u32[]{:S(2)}) copy-start(bf16[272,128]{1,0:T(8,128)(2,1)} %first_sums.1.refs_0_) | copy-start | bytes 208900
  2.7 7.7 %collective-permute-start.2 = (bf16[272,128]{1,0:T(8,128)(2,1)}, bf16[272,128]{1,0:T(8,128)(2,1)S(1)}, u32[]{:S(2)}, u32[]{:S(2)}) collective-permute-start(bf16[272,128]{1,0:T(8,128)(2,1)} %first_sums.1.refs_0_), channel_id=1, source_target_pairs={{0,8},{4,12},{8,0},{12,4},{1,9},{5,13},{9,1},{13,5},{2,10},{6,14},... | collective-permute-start | bytes 208904 | tf_op jit(solution)/shard_map/ppermute | solution.py:517
  2.8 12.7 %collective-permute-start.1 = (bf16[272,128]{1,0:T(8,128)(2,1)}, bf16[272,128]{1,0:T(8,128)(2,1)S(1)}, u32[]{:S(2)}, u32[]{:S(2)}) collective-permute-start(bf16[272,128]{1,0:T(8,128)(2,1)} %first_sums.1.refs_0_), channel_id=1, source_target_pairs={{0,12},{4,8},{8,4},{12,0},{1,13},{5,9},{9,5},{13,1},{2,14},{6,10},... | collective-permute-start | bytes 208904 | tf_op jit(solution)/shard_map/ppermute | solution.py:517
  5.8 9.7 %collective-permute-start = (bf16[272,128]{1,0:T(8,128)(2,1)}, bf16[272,128]{1,0:T(8,128)(2,1)S(1)}, u32[]{:S(2)}, u32[]{:S(2)}) collective-permute-start(bf16[272,128]{1,0:T(8,128)(2,1)} %first_sums.1.refs_0_), channel_id=1, source_target_pairs={{0,4},{4,0},{8,12},{12,8},{1,5},{5,1},{9,13},{13,9},{2,6},{6,2},{1... | collective-permute-start | bytes 208904 | tf_op jit(solution)/shard_map/ppermute | solution.py:517
  8.2 10.5 %collective-permute-start.5 = (bf16[256,128]{1,0:T(8,128)(2,1)S(1)}, bf16[256,128]{1,0:T(8,128)(2,1)S(1)}, u32[]{:S(2)}, u32[]{:S(2)}) collective-permute-start(bf16[256,128]{1,0:T(8,128)(2,1)S(1)} %second_sums.1.refs_4_), channel_id=1, source_target_pairs={{0,8},{4,12},{8,0},{12,4},{1,9},{5,13},{9,1},{13,5},{2,10},{6,14},... | collective-permute-start | bytes 196616 | tf_op jit(solution)/shard_map/ppermute | solution.py:517
  8.3 10.3 %collective-permute-start.4 = (bf16[256,128]{1,0:T(8,128)(2,1)S(1)}, bf16[256,128]{1,0:T(8,128)(2,1)S(1)}, u32[]{:S(2)}, u32[]{:S(2)}) collective-permute-start(bf16[256,128]{1,0:T(8,128)(2,1)S(1)} %second_sums.1.refs_4_), channel_id=1, source_target_pairs={{0,12},{4,8},{8,4},{12,0},{1,13},{5,9},{9,5},{13,1},{2,14},{6,10},... | collective-permute-start | bytes 196616 | tf_op jit(solution)/shard_map/ppermute | solution.py:517
  10.4 8.3 %collective-permute-start.3 = (bf16[256,128]{1,0:T(8,128)(2,1)S(1)}, bf16[256,128]{1,0:T(8,128)(2,1)S(1)}, u32[]{:S(2)}, u32[]{:S(2)}) collective-permute-start(bf16[256,128]{1,0:T(8,128)(2,1)S(1)} %second_sums.1.refs_4_), channel_id=1, source_target_pairs={{0,4},{4,0},{8,12},{12,8},{1,5},{5,1},{9,13},{13,9},{2,6},{6,2},{1... | collective-permute-start | bytes 196616 | tf_op jit(solution)/shard_map/ppermute | solution.py:517
  15.6 3.8 %copy-start.3 = (bf16[3,256,256]{2,1,0:T(8,128)(2,1)S(1)}, bf16[3,256,256]{2,1,0:T(8,128)(2,1)}, u32[]{:S(2)}) copy-start(bf16[3,256,256]{2,1,0:T(8,128)(2,1)} %constant.4.clone.refs_11_) | copy-start | bytes 1179652
  15.6 3.8 %copy-start.4 = (bf16[2,192,80]{2,1,0:T(8,128)(2,1)S(1)}, bf16[2,192,80]{2,1,0:T(8,128)(2,1)}, u32[]{:S(2)}) copy-start(bf16[2,192,80]{2,1,0:T(8,128)(2,1)} %constant.5.clone.refs_10_) | copy-start | bytes 184324
  15.6 3.8 %collective-permute-start.6 = (bf16[2,16,256]{2,1,0:T(8,128)(2,1)S(1)}, bf16[2,16,256]{2,1,0:T(8,128)(2,1)S(1)}, u32[]{:S(2)}, u32[]{:S(2)}) collective-permute-start(bf16[2,16,256]{2,1,0:T(8,128)(2,1)S(1)} %get-tuple-element.10), channel_id=1, source_target_pairs={{0,2},{2,0},{1,3},{3,1},{4,6},{6,4},{5,7},{7,5},{8,10},{10,8},{9,1... | collective-permute-start | bytes 49160 | tf_op jit(solution)/shard_map/ppermute | solution.py:558
  21.3 1.5 %copy-start.7 = (s32[4]{0:T(128)S(1)}, s32[4]{0:T(128)}, u32[]{:S(2)}) copy-start(s32[4]{0:T(128)} %owner_ref.1) | copy-start | bytes 52
  21.3 3.7 %collective-permute-start.7 = (f32[16,128]{1,0:T(8,128)S(1)}, f32[16,128]{1,0:T(8,128)S(1)}, u32[]{:S(2)}, u32[]{:S(2)}) collective-permute-start(f32[16,128]{1,0:T(8,128)S(1)} %get-tuple-element.13.after_ref.refs_0_), channel_id=1, source_target_pairs={{0,2},{2,0},{1,3},{3,1},{4,6},{6,4},{5,7},{7,5},{8,10},{10,8},{9,1... | collective-permute-start | bytes 24584 | tf_op jit(solution)/shard_map/ppermute | solution.py:585

commit v5 on v4

--- a/solution.py
+++ b/solution.py
@@ -388,11 +388,9 @@
         total = total + ref[...]
     pieces = total.shape[0]
     lanes = lax.broadcasted_iota(jnp.int32, (pieces, 128), 1)
-    starts = lanes % TILE == 0
     table = []
     for c in range(BASES + 1):
         line = total if c == 0 else pltpu.roll(total, 128 - c, 1)
-        line = jnp.where(starts, line, 0.0)
         if c < BASES:
             line = line + jnp.where(lanes == c * TILE, 1.0, 0.0)
         table.append(line)

time: 26.8 us -> 26.8 us (level)
  no operation moved by 1% of the time
where the time goes in v5:
time: 26.8 us; the launch traced here: 26.7 us
  starting transfers between devices  13.4 us (50%)
  Pallas kernels  9.41 us (35%)
  waiting for transfers between devices  3.06 us (11%)
  between operations  0.75 us (3%)
    ppermute x6, starting transfers between devices, everyone(): lax.ppermute(value, 'visit', [(i, i ^ shift) for i in range(visits)])  10.3 us
    pallas_call x7, Pallas kernels, call(): pl.pallas_call(kernel, out_shape=outs, in_specs=in_specs, out_specs=out_s...  9.41 us
    ppermute x1, starting transfers between devices, body(): halo = lax.ppermute(edge, 'strip', [(0, 1), (1, 0)])  1.56 us
    ppermute x1, starting transfers between devices, body(): totals = [sums, lax.ppermute(sums, 'strip', [(0, 1), (1, 0)])]  1.51 us
    ppermute x6, waiting for transfers between devices, everyone(): lax.ppermute(value, 'visit', [(i, i ^ shift) for i in range(visits)])  1.45 us
    ppermute x1, waiting for transfers between devices, body(): totals = [sums, lax.ppermute(sums, 'strip', [(0, 1), (1, 0)])]  0.87 us
    ppermute x1, waiting for transfers between devices, body(): halo = lax.ppermute(edge, 'strip', [(0, 1), (1, 0)])  0.75 us
  transfers between devices with their start and end apart: 8, of which 3 were waited for; matrix products, arithmetic and copies ran while one was open for 0% of the time, Pallas kernels for 14%

profile of v5, /device:TPU:16, one launch (start us, length us, event | category | flops | bytes accessed | tf_op | source)
XLA Modules:
  0.0 26.7 jit_solution(13326239579832416573)
XLA Ops:
  0.7 2.0 %first_sums.1.refs_0_ = bf16[272,128]{1,0:T(8,128)(2,1)} custom-call(s32[16]{0:T(128)} %bitcast.12, bf16[1,16]{1,0:T(2,128)(2,1)} %weight_ref.1, bf16[16,64,256]{2,1,0:T(8,128)(2,1)} %bitcast.8, s32[16,64,256]{2,1,0:T(8,128)} %bitcast.5), custom_call_target="tpu_custom_call" | custom-call | bytes 2097152 | tf_op jit(solution)/shard_map/first_sums/pallas_call | solution.py:454
  2.7 0.0 copy-start.2
  2.7 0.1 collective-permute-start.2
  2.8 3.0 %collective-permute-start.1 = (bf16[272,128]{1,0:T(8,128)(2,1)}, bf16[272,128]{1,0:T(8,128)(2,1)S(1)}, u32[]{:S(2)}, u32[]{:S(2)}) collective-permute-start(bf16[272,128]{1,0:T(8,128)(2,1)} %first_sums.1.refs_0_), channel_id=1, source_target_pairs={{0,12},{4,8},{8,4},{12,0},{1,13},{5,9},{9,5},{13,1},{2,14},{6,10},... | collective-permute-start | bytes 208904 | tf_op jit(solution)/shard_map/ppermute | solution.py:515
  5.8 1.3 %collective-permute-start = (bf16[272,128]{1,0:T(8,128)(2,1)}, bf16[272,128]{1,0:T(8,128)(2,1)S(1)}, u32[]{:S(2)}, u32[]{:S(2)}) collective-permute-start(bf16[272,128]{1,0:T(8,128)(2,1)} %first_sums.1.refs_0_), channel_id=1, source_target_pairs={{0,4},{4,0},{8,12},{12,8},{1,5},{5,1},{9,13},{13,9},{2,6},{6,2},{1... | collective-permute-start | bytes 208904 | tf_op jit(solution)/shard_map/ppermute | solution.py:515
  7.2 1.0 %second_sums.1.refs_4_ = bf16[256,128]{1,0:T(8,128)(2,1)S(1)} custom-call(s32[16]{0:T(128)S(1)} %bitcast.13, bf16[1,16]{1,0:T(2,128)(2,1)S(1)} %copy-done.6, bf16[16,64,256]{2,1,0:T(8,128)(2,1)S(1)} %bitcast.9, s32[16,64,256]{2,1,0:T(8,128)S(1)} %bitcast.6), custom_call_target="tpu_custom_call" | custom-call | bytes 1048576 | tf_op jit(solution)/shard_map/second_sums/pallas_call | solution.py:454
  8.2 0.2 collective-permute-start.5
  8.3 2.0 %collective-permute-start.4 = (bf16[256,128]{1,0:T(8,128)(2,1)S(1)}, bf16[256,128]{1,0:T(8,128)(2,1)S(1)}, u32[]{:S(2)}, u32[]{:S(2)}) collective-permute-start(bf16[256,128]{1,0:T(8,128)(2,1)S(1)} %second_sums.1.refs_4_), channel_id=1, source_target_pairs={{0,12},{4,8},{8,4},{12,0},{1,13},{5,9},{9,5},{13,1},{2,14},{6,10},... | collective-permute-start | bytes 196616 | tf_op jit(solution)/shard_map/ppermute | solution.py:515
  10.4 0.0 collective-permute-done.2.refs_3_
  10.4 3.7 %collective-permute-start.3 = (bf16[256,128]{1,0:T(8,128)(2,1)S(1)}, bf16[256,128]{1,0:T(8,128)(2,1)S(1)}, u32[]{:S(2)}, u32[]{:S(2)}) collective-permute-start(bf16[256,128]{1,0:T(8,128)(2,1)S(1)} %second_sums.1.refs_4_), channel_id=1, source_target_pairs={{0,4},{4,0},{8,12},{12,8},{1,5},{5,1},{9,13},{13,9},{2,6},{6,2},{1... | collective-permute-start | bytes 196616 | tf_op jit(solution)/shard_map/ppermute | solution.py:515
  14.0 1.4 %collective-permute-done.1.refs_2_ = bf16[272,128]{1,0:T(8,128)(2,1)S(1)} collective-permute-done((bf16[272,128]{1,0:T(8,128)(2,1)}, bf16[272,128]{1,0:T(8,128)(2,1)S(1)}, u32[]{:S(2)}, u32[]{:S(2)}) %collective-permute-start.1) | collective-permute-done | bytes 69664 | tf_op jit(solution)/shard_map/ppermute | solution.py:515
  15.5 0.0 collective-permute-done.refs_1_
  15.5 0.1 border.1
  15.6 0.0 copy-start.3
  15.6 0.0 copy-start.4
  15.6 1.6 %collective-permute-start.6 = (bf16[2,16,256]{2,1,0:T(8,128)(2,1)S(1)}, bf16[2,16,256]{2,1,0:T(8,128)(2,1)S(1)}, u32[]{:S(2)}, u32[]{:S(2)}) collective-permute-start(bf16[2,16,256]{2,1,0:T(8,128)(2,1)S(1)} %get-tuple-element.10), channel_id=1, source_target_pairs={{0,2},{2,0},{1,3},{3,1},{4,6},{6,4},{5,7},{7,5},{8,10},{10,8},{9,1... | collective-permute-start | bytes 49160 | tf_op jit(solution)/shard_map/ppermute | solution.py:556
  17.2 1.5 %sorted_usable.1 = (bf16[2,128,1024]{2,1,0:T(8,128)(2,1)S(1)}, bf16[2,128,1024]{2,1,0:T(8,128)(2,1)S(1)}, s32[16]{0:T(128)S(1)}) custom-call(s32[16]{0:T(128)S(1)} %bitcast.14, bf16[16,64,256]{2,1,0:T(8,128)(2,1)S(1)} %bitcast.10, s32[16,64,256]{2,1,0:T(8,128)S(1)} %bitcast.7), custom_call_target="tpu_custom_call" | custom-call | bytes 3145728 | tf_op jit(solution)/shard_map/sorted_usable/pallas_call | solution.py:454
  18.6 0.0 collective-permute-done.5.refs_7_
  18.7 0.7 %collective-permute-done.6.refs_9_ = bf16[2,16,256]{2,1,0:T(8,128)(2,1)S(1)} collective-permute-done((bf16[2,16,256]{2,1,0:T(8,128)(2,1)S(1)}, bf16[2,16,256]{2,1,0:T(8,128)(2,1)S(1)}, u32[]{:S(2)}, u32[]{:S(2)}) %collective-permute-start.6) | collective-permute-done | bytes 16416 | tf_op jit(solution)/shard_map/ppermute | solution.py:556
  19.4 1.9 %normal_equations.1 = (bf16[2,96,1024]{2,1,0:T(8,128)(2,1)S(1)}, f32[16,128]{1,0:T(8,128)S(1)}) custom-call(bf16[272,128]{1,0:T(8,128)(2,1)S(1)} %copy-done.2, bf16[272,128]{1,0:T(8,128)(2,1)S(1)} %collective-permute-done.refs_1_, bf16[272,128]{1,0:T(8,128)(2,1)S(1)} %collective-permute-done.1.refs_2_, bf16[272,128]{1,0:T(8,128)(2,1)S(1)} %collective-permute-done.2.refs_3_, ...), custom_call_target="tpu_custom_call" | custom-call | bytes 2097152 | tf_op jit(solution)/shard_map/normal_equations/pallas_call | solution.py:454
  21.3 1.5 %collective-permute-start.7 = (f32[16,128]{1,0:T(8,128)S(1)}, f32[16,128]{1,0:T(8,128)S(1)}, u32[]{:S(2)}, u32[]{:S(2)}) collective-permute-start(f32[16,128]{1,0:T(8,128)S(1)} %get-tuple-element.13.after_ref.refs_0_), channel_id=1, source_target_pairs={{0,2},{2,0},{1,3},{3,1},{4,6},{6,4},{5,7},{7,5},{8,10},{10,8},{9,1... | collective-permute-start | bytes 24584 | tf_op jit(solution)/shard_map/ppermute | solution.py:583
  22.8 1.3 %own_patch.1 = bf16[64,256]{1,0:T(8,128)(2,1)} custom-call(s32[4]{0:T(128)S(1)} %copy-done.7, f32[16,128]{1,0:T(8,128)S(1)} %get-tuple-element.13.after_ref.refs_0_, bf16[272,128]{1,0:T(8,128)(2,1)S(1)} %copy-done.2, bf16[272,128]{1,0:T(8,128)(2,1)S(1)} %collective-permute-done.refs_1_, bf16[272,128]{1,0:T(8,128)(2,1)S(1)} %collective-permute-done.1.refs_2_, ...), custom_call_target="tpu_custom_call" | custom-call | bytes 1048576 | tf_op jit(solution)/shard_map/own_patch/pallas_call | solution.py:454
  24.1 0.9 %collective-permute-done.7.refs_1_ = f32[16,128]{1,0:T(8,128)S(1)} collective-permute-done((f32[16,128]{1,0:T(8,128)S(1)}, f32[16,128]{1,0:T(8,128)S(1)}, u32[]{:S(2)}, u32[]{:S(2)}) %collective-permute-start.7) | collective-permute-done | bytes 8224 | tf_op jit(solution)/shard_map/ppermute | solution.py:583
  25.0 1.7 %fit.1 = bf16[16,64,256]{2,1,0:T(8,128)(2,1)} custom-call(s32[16]{0:T(128)S(1)} %get-tuple-element.14.order_any, f32[16,128]{1,0:T(8,128)S(1)} %get-tuple-element.13.after_ref.refs_0_, f32[16,128]{1,0:T(8,128)S(1)} %collective-permute-done.7.refs_1_, bf16[2,96,1024]{2,1,0:T(8,128)(2,1)S(1)} %get-tuple-element.15.refs_2_, bf16[16,64,256]{2,1,0:T(8,128)(2,1)S(1)} %bitcast.11), custom_call_target="tpu_custom_call" | custom-call | bytes 2097152 | tf_op jit(solution)/shard_map/fit/pallas_call | solution.py:454
  (15 shorter events, 0.0 us)
Async XLA Ops:
  0.6 6.5 %copy-start = (s32[1,16,64,256]{3,2,1,0:T(8,128)S(1)}, s32[1,16,64,256]{3,2,1,0:T(8,128)}, u32[]{:S(2)}) copy-start(s32[1,16,64,256]{3,2,1,0:T(8,128)} %param.8) | copy-start | bytes 3145732
  0.6 6.5 %copy-start.1 = (bf16[1,16,64,256]{3,2,1,0:T(8,128)(2,1)S(1)}, bf16[1,16,64,256]{3,2,1,0:T(8,128)(2,1)}, u32[]{:S(2)}) copy-start(bf16[1,16,64,256]{3,2,1,0:T(8,128)(2,1)} %param.7) | copy-start | bytes 1572868
  0.7 6.5 %copy-start.5 = (s32[16,1]{0,1:T(1,128)S(1)}, s32[16,1]{0,1:T(1,128)}, u32[]{:S(2)}) copy-start(s32[16,1]{0,1:T(1,128)} %param.10) | copy-start | bytes 196
  0.7 6.5 %copy-start.6 = (bf16[1,16]{1,0:T(2,128)(2,1)S(1)}, bf16[1,16]{1,0:T(2,128)(2,1)}, u32[]{:S(2)}) copy-start(bf16[1,16]{1,0:T(2,128)(2,1)} %weight_ref.1) | copy-start | bytes 100
  2.7 12.8 %copy-start.2 = (bf16[272,128]{1,0:T(8,128)(2,1)S(1)}, bf16[272,128]{1,0:T(8,128)(2,1)}, u32[]{:S(2)}) copy-start(bf16[272,128]{1,0:T(8,128)(2,1)} %first_sums.1.refs_0_) | copy-start | bytes 208900
  2.7 7.7 %collective-permute-start.2 = (bf16[272,128]{1,0:T(8,128)(2,1)}, bf16[272,128]{1,0:T(8,128)(2,1)S(1)}, u32[]{:S(2)}, u32[]{:S(2)}) collective-permute-start(bf16[272,128]{1,0:T(8,128)(2,1)} %first_sums.1.refs_0_), channel_id=1, source_target_pairs={{0,8},{4,12},{8,0},{12,4},{1,9},{5,13},{9,1},{13,5},{2,10},{6,14},... | collective-permute-start | bytes 208904 | tf_op jit(solution)/shard_map/ppermute | solution.py:515
  2.8 12.7 %collective-permute-start.1 = (bf16[272,128]{1,0:T(8,128)(2,1)}, bf16[272,128]{1,0:T(8,128)(2,1)S(1)}, u32[]{:S(2)}, u32[]{:S(2)}) collective-permute-start(bf16[272,128]{1,0:T(8,128)(2,1)} %first_sums.1.refs_0_), channel_id=1, source_target_pairs={{0,12},{4,8},{8,4},{12,0},{1,13},{5,9},{9,5},{13,1},{2,14},{6,10},... | collective-permute-start | bytes 208904 | tf_op jit(solution)/shard_map/ppermute | solution.py:515
  5.8 9.7 %collective-permute-start = (bf16[272,128]{1,0:T(8,128)(2,1)}, bf16[272,128]{1,0:T(8,128)(2,1)S(1)}, u32[]{:S(2)}, u32[]{:S(2)}) collective-permute-start(bf16[272,128]{1,0:T(8,128)(2,1)} %first_sums.1.refs_0_), channel_id=1, source_target_pairs={{0,4},{4,0},{8,12},{12,8},{1,5},{5,1},{9,13},{13,9},{2,6},{6,2},{1... | collective-permute-start | bytes 208904 | tf_op jit(solution)/shard_map/ppermute | solution.py:515
  8.2 10.5 %collective-permute-start.5 = (bf16[256,128]{1,0:T(8,128)(2,1)S(1)}, bf16[256,128]{1,0:T(8,128)(2,1)S(1)}, u32[]{:S(2)}, u32[]{:S(2)}) collective-permute-start(bf16[256,128]{1,0:T(8,128)(2,1)S(1)} %second_sums.1.refs_4_), channel_id=1, source_target_pairs={{0,8},{4,12},{8,0},{12,4},{1,9},{5,13},{9,1},{13,5},{2,10},{6,14},... | collective-permute-start | bytes 196616 | tf_op jit(solution)/shard_map/ppermute | solution.py:515
  8.3 10.3 %collective-permute-start.4 = (bf16[256,128]{1,0:T(8,128)(2,1)S(1)}, bf16[256,128]{1,0:T(8,128)(2,1)S(1)}, u32[]{:S(2)}, u32[]{:S(2)}) collective-permute-start(bf16[256,128]{1,0:T(8,128)(2,1)S(1)} %second_sums.1.refs_4_), channel_id=1, source_target_pairs={{0,12},{4,8},{8,4},{12,0},{1,13},{5,9},{9,5},{13,1},{2,14},{6,10},... | collective-permute-start | bytes 196616 | tf_op jit(solution)/shard_map/ppermute | solution.py:515
  10.4 8.3 %collective-permute-start.3 = (bf16[256,128]{1,0:T(8,128)(2,1)S(1)}, bf16[256,128]{1,0:T(8,128)(2,1)S(1)}, u32[]{:S(2)}, u32[]{:S(2)}) collective-permute-start(bf16[256,128]{1,0:T(8,128)(2,1)S(1)} %second_sums.1.refs_4_), channel_id=1, source_target_pairs={{0,4},{4,0},{8,12},{12,8},{1,5},{5,1},{9,13},{13,9},{2,6},{6,2},{1... | collective-permute-start | bytes 196616 | tf_op jit(solution)/shard_map/ppermute | solution.py:515
  15.6 3.8 %copy-start.3 = (bf16[3,256,256]{2,1,0:T(8,128)(2,1)S(1)}, bf16[3,256,256]{2,1,0:T(8,128)(2,1)}, u32[]{:S(2)}) copy-start(bf16[3,256,256]{2,1,0:T(8,128)(2,1)} %constant.4.clone.refs_11_) | copy-start | bytes 1179652
  15.6 3.8 %copy-start.4 = (bf16[2,192,80]{2,1,0:T(8,128)(2,1)S(1)}, bf16[2,192,80]{2,1,0:T(8,128)(2,1)}, u32[]{:S(2)}) copy-start(bf16[2,192,80]{2,1,0:T(8,128)(2,1)} %constant.5.clone.refs_10_) | copy-start | bytes 184324
  15.6 3.8 %collective-permute-start.6 = (bf16[2,16,256]{2,1,0:T(8,128)(2,1)S(1)}, bf16[2,16,256]{2,1,0:T(8,128)(2,1)S(1)}, u32[]{:S(2)}, u32[]{:S(2)}) collective-permute-start(bf16[2,16,256]{2,1,0:T(8,128)(2,1)S(1)} %get-tuple-element.10), channel_id=1, source_target_pairs={{0,2},{2,0},{1,3},{3,1},{4,6},{6,4},{5,7},{7,5},{8,10},{10,8},{9,1... | collective-permute-start | bytes 49160 | tf_op jit(solution)/shard_map/ppermute | solution.py:556
  21.3 1.5 %copy-start.7 = (s32[4]{0:T(128)S(1)}, s32[4]{0:T(128)}, u32[]{:S(2)}) copy-start(s32[4]{0:T(128)} %owner_ref.1) | copy-start | bytes 52
  21.3 3.7 %collective-permute-start.7 = (f32[16,128]{1,0:T(8,128)S(1)}, f32[16,128]{1,0:T(8,128)S(1)}, u32[]{:S(2)}, u32[]{:S(2)}) collective-permute-start(f32[16,128]{1,0:T(8,128)S(1)} %get-tuple-element.13.after_ref.refs_0_), channel_id=1, source_target_pairs={{0,2},{2,0},{1,3},{3,1},{4,6},{6,4},{5,7},{7,5},{8,10},{10,8},{9,1... | collective-permute-start | bytes 24584 | tf_op jit(solution)/shard_map/ppermute | solution.py:583
